TPU v7x, 32 devices: a whole 2x2x4 slice. The times are simulated.
32 devices in a mesh: dp: 8 (over z, y), tensor: 4 (over x, core).
Axes of the slice: x: 2, y: 2, z: 4, core: 2. Of those that a mesh axis runs over, the one named last changes fastest.
Arguments:
- token_ids: int32 [8192], P('dp'), may hold values from 0 to 31999
- lengths: int32 [32], P('dp'), may hold values from 0 to 1024, as said below
- time_steps: int32 [32], P('dp'), may hold values from 0 to 999
- embed_table: bfloat16 [32000, 256], P(('dp', 'tensor')), may hold values from -6 to 6
- input_weight: bfloat16 [256, 1024], P('dp'), may hold values from -0.375 to 0.375
- time_weight: bfloat16 [256, 4096], P('dp'), may hold values from -0.375 to 0.375
- project_weight: bfloat16 [1024, 3072], P('dp', 'tensor'), may hold values from -0.1875 to 0.1875
- output_weight: bfloat16 [1024, 1024], P('tensor', 'dp'), may hold values from -1.5 to 1.5
- up_weight: bfloat16 [1024, 4096], P('dp', 'tensor'), may hold values from -0.25 to 0.25
- down_weight: bfloat16 [4096, 1024], P('tensor', 'dp'), may hold values from -0.125 to 0.125
- cotangent: bfloat16 [8192, 1024], P('dp'), may hold values from -6 to 6
Outputs:
- block_out: bfloat16 [8192, 1024], P('dp')
- grad_table: float32 [32000, 256], P(('dp', 'tensor'))
- grad_input: float32 [256, 1024], P('dp')
- grad_time: float32 [256, 4096], P('dp')
- grad_project: float32 [1024, 3072], P('dp', 'tensor')
- grad_output: float32 [1024, 1024], P('tensor', 'dp')
- grad_up: float32 [1024, 4096], P('dp', 'tensor')
- grad_down: float32 [4096, 1024], P('tensor', 'dp')
Inputs may be any that keep to these rules, and one draw needn't show every extreme that they name: The 4 lengths of each pack, in order, fill its 1024 rows exactly; a length may be zero; in every draw some pack is a single document of 1024 rows.
All inputs are finite; a program needn't handle non-finite values.
Results may differ from a plain program's by a relative error of at most 0.017.
Values may be sent and summed in bfloat16 or wider, within the bound.
No kernel may reach another device: no remote copies, remote signals or barrier semaphores. Data moves between devices by JAX's collectives and lax.ppermute only.
A program may use at most 256 MiB of HBM per device.

v0:
```python
import math

import jax
import jax.numpy as jnp
from jax import lax
from jax.sharding import PartitionSpec as P

HD = 64
EMB = 256


table_eps = 1e-06
norm_eps = 1e-05
masked_score = -1e30
highest = lax.Precision.HIGHEST


def normalize(table_rows):
    return table_rows * lax.rsqrt(
        jnp.mean(table_rows * table_rows, axis=1, keepdims=True) + table_eps
    )


def layer_norm(value, scale, shift):
    centred = value - jnp.mean(value, axis=-1, keepdims=True)
    return (
        centred
        * lax.rsqrt(jnp.mean(centred * centred, axis=-1, keepdims=True) + norm_eps)
        * (1.0 + scale)
        + shift
    )


def time_features(step_index, width):
    half = width // 2
    frequency = jnp.exp(-math.log(10000.0) * jnp.arange(half).astype(jnp.float32) / half)
    angles = step_index.astype(jnp.float32)[:, None] * frequency[None, :]
    return jnp.concatenate([jnp.sin(angles), jnp.cos(angles)], axis=1)


def gelu_exact(value):
    return jax.nn.gelu(value, approximate=False)


def per_device(
    token_ids,
    lengths,
    time_steps,
    embed_table,
    input_weight,
    time_weight,
    project_weight,
    output_weight,
    up_weight,
    down_weight,
    cotangent,
):
    rows = token_ids.shape[0]
    groups = lax.axis_size("tensor")
    tensor_place = lax.axis_index("tensor")
    shard_rows = embed_table.shape[0]
    factor = 1.0 / math.sqrt(HD)
    normed, normed_back = jax.vjp(normalize, embed_table.astype(jnp.float32))
    normed_low = normed.astype(jnp.bfloat16)
    gathered = (
        lax.all_gather(input_weight, "dp", axis=0, tiled=True),
        lax.all_gather(time_weight, "dp", axis=0, tiled=True),
        lax.all_gather(project_weight, "dp", axis=0, tiled=True),
        lax.all_gather(output_weight, "dp", axis=1, tiled=True),
        lax.all_gather(up_weight, "dp", axis=0, tiled=True),
        lax.all_gather(down_weight, "dp", axis=1, tiled=True),
    )
    input_full, time_full, project_full, output_full, up_full, down_full = gathered

    def vocab_rows(count):
        flat_index = jnp.arange(count, dtype=jnp.int32)
        return (
            flat_index // shard_rows * groups + tensor_place
        ) * shard_rows + flat_index % shard_rows

    token_block = min(256, rows)
    piece = lax.all_gather(normed_low, "dp", axis=0, tiled=True)
    vocab = vocab_rows(piece.shape[0])
    parts = []
    for add_begin in range(0, rows, token_block):
        add_onehot = (
            token_ids[add_begin : add_begin + token_block, None] == vocab[None, :]
        ).astype(jnp.bfloat16)
        parts.append(jnp.dot(add_onehot, piece, preferred_element_type=jnp.float32))
    partial_embed = jnp.concatenate(parts, axis=0)
    embed = lax.psum(partial_embed.astype(jnp.bfloat16), "tensor")
    stream_zero = jnp.dot(embed, input_full, preferred_element_type=jnp.float32)
    ends = jnp.cumsum(lengths)
    position = jnp.arange(rows, dtype=jnp.int32)
    document = jnp.sum((position[:, None] >= ends[None, :]).astype(jnp.int32), axis=1)
    member = (document[:, None] == jnp.arange(lengths.shape[0], dtype=jnp.int32)[None, :]).astype(
        jnp.float32
    )
    features = time_features(time_steps, EMB).astype(jnp.bfloat16)
    modulation = jnp.dot(features, time_full, preferred_element_type=jnp.float32)
    row_mods = jnp.dot(member, modulation, precision=highest)
    scale_one, shift_one, scale_two, shift_two = jnp.split(row_mods, 4, axis=1)
    normed_one, norm_one_back = jax.vjp(layer_norm, stream_zero, scale_one, shift_one)
    hidden_one = normed_one.astype(jnp.bfloat16)
    projected = jnp.dot(hidden_one, project_full, preferred_element_type=jnp.float32).astype(
        jnp.bfloat16
    )
    heads_here = projected.shape[1] // (3 * HD)
    projected = projected.reshape(rows, heads_here, 3, HD)
    query = jnp.transpose(projected[:, :, 0], (1, 0, 2))
    keys = jnp.transpose(projected[:, :, 1], (1, 0, 2))
    values = jnp.transpose(projected[:, :, 2], (1, 0, 2))
    query_block = min(512, rows)

    def scores_of(begin):
        block_query = query[:, begin : begin + query_block]
        plain = (
            jnp.einsum("hqd,hkd->hqk", block_query, keys, preferred_element_type=jnp.float32)
            * factor
        )
        allowed = document[begin : begin + query_block, None] == document[None, :]
        return (jnp.where(allowed[None], plain, masked_score), block_query)

    outputs = []
    logsums = []
    kept_probs = []
    for begin in range(0, rows, query_block):
        scores, block_query = scores_of(begin)
        peak = jnp.max(scores, axis=2, keepdims=True)
        expo = jnp.exp(scores - peak)
        total = jnp.sum(expo, axis=2, keepdims=True)
        logsums.append(peak + jnp.log(total))
        probs_low = (expo / total).astype(jnp.bfloat16)
        kept_probs.append(probs_low)
        outputs.append(
            jnp.einsum("hqk,hkd->hqd", probs_low, values, preferred_element_type=jnp.float32)
        )
    attended = (
        jnp.transpose(jnp.concatenate(outputs, axis=1), (1, 0, 2))
        .reshape(rows, heads_here * HD)
        .astype(jnp.bfloat16)
    )
    attention_sum = lax.psum(
        jnp.dot(attended, output_full, preferred_element_type=jnp.float32), "tensor"
    )
    stream_one_rows = stream_zero + attention_sum
    normed_two, norm_two_back = jax.vjp(layer_norm, stream_one_rows, scale_two, shift_two)
    hidden_two = normed_two.astype(jnp.bfloat16)
    upward = jnp.dot(hidden_two, up_full, preferred_element_type=jnp.float32)
    activated, gelu_back = jax.vjp(gelu_exact, upward)
    activated_low = activated.astype(jnp.bfloat16)
    branch = lax.psum(
        jnp.dot(activated_low, down_full, preferred_element_type=jnp.float32), "tensor"
    )
    block_out = (stream_one_rows + branch).astype(jnp.bfloat16)
    grad_down = jnp.dot(activated_low.T, cotangent, preferred_element_type=jnp.float32)
    grad_active = jnp.dot(cotangent, down_full.T, preferred_element_type=jnp.float32)
    grad_upward = gelu_back(grad_active)[0].astype(jnp.bfloat16)
    grad_up = jnp.dot(hidden_two.T, grad_upward, preferred_element_type=jnp.float32)
    grad_hidden_two = lax.psum(
        jnp.dot(grad_upward, up_full.T, preferred_element_type=jnp.float32), "tensor"
    )
    grad_stream_rows, grad_scale_two, grad_shift_two = norm_two_back(grad_hidden_two)
    grad_stream_rows = grad_stream_rows + cotangent.astype(jnp.float32)
    grad_attn_rows = grad_stream_rows.astype(jnp.bfloat16)
    grad_output = jnp.dot(attended.T, grad_attn_rows, preferred_element_type=jnp.float32)
    grad_attended = jnp.dot(
        grad_attn_rows, output_full.T, preferred_element_type=jnp.float32
    ).astype(jnp.bfloat16)
    grad_attended = jnp.transpose(grad_attended.reshape(rows, heads_here, HD), (1, 0, 2))
    query_grads = []
    grad_keys = jnp.zeros(keys.shape, jnp.float32)
    grad_values = jnp.zeros(values.shape, jnp.float32)
    for number, begin in enumerate(range(0, rows, query_block)):
        scores, block_query = scores_of(begin)
        probs = jnp.exp(scores - logsums[number])
        block_grad = grad_attended[:, begin : begin + query_block]
        grad_probs = jnp.einsum(
            "hqd,hkd->hqk", block_grad, values, preferred_element_type=jnp.float32
        )
        inner = jnp.sum(probs * grad_probs, axis=2, keepdims=True)
        grad_scores = (probs * (grad_probs - inner)).astype(jnp.bfloat16)
        query_grads.append(
            jnp.einsum("hqk,hkd->hqd", grad_scores, keys, preferred_element_type=jnp.float32)
            * factor
        )
        grad_keys = (
            grad_keys
            + jnp.einsum(
                "hqk,hqd->hkd", grad_scores, block_query, preferred_element_type=jnp.float32
            )
            * factor
        )
        grad_values = grad_values + jnp.einsum(
            "hqk,hqd->hkd", kept_probs[number], block_grad, preferred_element_type=jnp.float32
        )
    grad_query = jnp.concatenate(query_grads, axis=1)
    grad_projected = jnp.stack([grad_query, grad_keys, grad_values], axis=2)
    grad_projected = (
        jnp.transpose(grad_projected, (1, 0, 2, 3))
        .reshape(rows, heads_here * 3 * HD)
        .astype(jnp.bfloat16)
    )
    grad_project = jnp.dot(hidden_one.T, grad_projected, preferred_element_type=jnp.float32)
    grad_hidden_one = lax.psum(
        jnp.dot(grad_projected, project_full.T, preferred_element_type=jnp.float32), "tensor"
    )
    grad_stream_zero, grad_scale_one, grad_shift_one = norm_one_back(grad_hidden_one)
    grad_zero_low = (grad_stream_zero + grad_stream_rows).astype(jnp.bfloat16)
    grad_rows = jnp.concatenate(
        [grad_scale_one, grad_shift_one, grad_scale_two, grad_shift_two], axis=1
    )
    partial_modulation = jnp.dot(member.T, grad_rows, precision=highest)
    grad_stream_zero = grad_zero_low
    grad_input = jnp.dot(embed.T, grad_stream_zero, preferred_element_type=jnp.float32)
    grad_embed = jnp.dot(grad_stream_zero, input_full.T, preferred_element_type=jnp.float32).astype(
        jnp.bfloat16
    )
    grad_time = jnp.dot(features.astype(jnp.float32).T, partial_modulation, precision=highest)
    every_row = shard_rows * lax.axis_size("dp")
    vocab_all = vocab_rows(every_row)
    grad_normed = jnp.zeros((every_row, EMB), jnp.float32)
    for begin in range(0, rows, token_block):
        onehot = (token_ids[begin : begin + token_block, None] == vocab_all[None, :]).astype(
            jnp.bfloat16
        )
        grad_normed = grad_normed + jnp.einsum(
            "tv,te->ve",
            onehot,
            grad_embed[begin : begin + token_block],
            preferred_element_type=jnp.float32,
        )
    (
        summed_input,
        summed_time,
        summed_project,
        summed_output,
        summed_up,
        summed_down,
        summed_table,
    ) = (
        lax.psum_scatter(grad_input, "dp", scatter_dimension=0, tiled=True),
        lax.psum_scatter(grad_time, "dp", scatter_dimension=0, tiled=True),
        lax.psum_scatter(grad_project, "dp", scatter_dimension=0, tiled=True),
        lax.psum_scatter(grad_output, "dp", scatter_dimension=1, tiled=True),
        lax.psum_scatter(grad_up, "dp", scatter_dimension=0, tiled=True),
        lax.psum_scatter(grad_down, "dp", scatter_dimension=1, tiled=True),
        lax.psum_scatter(grad_normed, "dp", scatter_dimension=0, tiled=True),
    )
    grad_table = normed_back(summed_table)[0]
    return (
        block_out,
        grad_table,
        summed_input,
        summed_time,
        summed_project,
        summed_output,
        summed_up,
        summed_down,
    )


def solution(mesh):
    return jax.shard_map(
        per_device,
        mesh=mesh,
        in_specs=(
            P("dp"),
            P("dp"),
            P("dp"),
            P(("dp", "tensor"), None),
            P("dp", None),
            P("dp", None),
            P("dp", "tensor"),
            P("tensor", "dp"),
            P("dp", "tensor"),
            P("tensor", "dp"),
            P("dp", None),
        ),
        out_specs=(
            P("dp", None),
            P(("dp", "tensor"), None),
            P("dp", None),
            P("dp", None),
            P("dp", "tensor"),
            P("tensor", "dp"),
            P("dp", "tensor"),
            P("tensor", "dp"),
        ),
        check_vma=False,
    )
```

profile of v0, /device:TPU:0, one launch (start us, length us, event | category | flops | bytes accessed | tf_op | source)
XLA Modules:
  0.0 1423.0 jit_solution(14659890896344070602)
XLA Ops:
  13.4 73.3 %all-gather.6.cloned.1.call-done = bf16[8000,256]{1,0:T(8,128)(2,1)} async-done(((bf16[1000,256]{1,0:T(8,128)(2,1)}), bf16[8000,256]{1,0:T(8,128)(2,1)}) %all-gather.6.cloned.1.call-update) | async-done | bytes 4096016 | tf_op jit(solution)/shard_map/all_gather | solution.py:82
  96.1 32.8 %all_gather.22 = bf16[256,1024]{1,0:T(8,128)(2,1)S(1)} all-gather(bf16[32,1024]{1,0:T(8,128)(2,1)S(1)} %copy-done.46), channel_id=1, replica_groups=mesh['dp'=8,'tensor'=4] {'dp'}, dimensions={0}, use_global_device_ids=true | all-gather | bytes 589824 | tf_op jit(solution)/shard_map/all_gather | solution.py:66
  129.0 30.1 %all_gather.25 = bf16[256,1024]{1,0:T(8,128)(2,1)} all-gather(bf16[256,128]{1,0:T(8,128)(2,1)S(1)} %copy-done.47), channel_id=1, replica_groups=mesh['dp'=8,'tensor'=4] {'dp'}, dimensions={1}, use_global_device_ids=true | all-gather | bytes 589824 | tf_op jit(solution)/shard_map/all_gather | solution.py:69
  161.9 11.1 fusion.75
  173.0 9.1 all-reduce.6.cloned.1.call-done
  191.0 37.4 %all-gather.10.cloned.1.call-done = bf16[1024,768]{1,0:T(8,128)(2,1)} async-done(((bf16[128,768]{1,0:T(8,128)(2,1)}), bf16[1024,768]{1,0:T(8,128)(2,1)}) %all-gather.10.cloned.1.call-update) | async-done | bytes 1572880 | tf_op jit(solution)/shard_map/all_gather | solution.py:68
  256.0 82.9 %all-reduce.8.cloned.1.call-done = f32[1024,1024]{0,1:T(8,128)} async-done(((f32[1024,1024]{0,1:T(8,128)}), f32[1024,1024]{0,1:T(8,128)}) %all-reduce.8.cloned.1.call-update) | async-done | bytes 4194320 | tf_op jit(solution)/shard_map/psum | solution.py:143
  350.5 40.0 %all-gather.12.cloned.1.call-done = bf16[1024,1024]{1,0:T(8,128)(2,1)} async-done(((bf16[128,1024]{1,0:T(8,128)(2,1)}), bf16[1024,1024]{1,0:T(8,128)(2,1)}) %all-gather.12.cloned.1.call-update) | async-done | bytes 2097168 | tf_op jit(solution)/shard_map/all_gather | solution.py:70
  396.6 45.9 %all-gather.14.cloned.1.call-done = bf16[1024,1024]{1,0:T(8,128)(2,1)} async-done(((bf16[1024,128]{1,0:T(8,128)(2,1)}), bf16[1024,1024]{1,0:T(8,128)(2,1)}) %all-gather.14.cloned.1.call-update) | async-done | bytes 2097168 | tf_op jit(solution)/shard_map/all_gather | solution.py:71
  442.4 15.2 %add_convert_fusion.1 = (bf16[1024,1024]{0,1:T(8,128)(2,1)S(1)}, f32[1024,1024]{0,1:T(8,128)}) fusion(f32[1024,1024]{0,1:T(8,128)} %fusion.126, bf16[1024,1024]{1,0:T(8,128)(2,1)} %param.21, bf16[1024,1024]{1,0:T(8,128)(2,1)} %all-gather.14.cloned.1.call-done), kind=kOutput, calls=%fused_computation.54 | convolution fusion | flops 2222981120 | bytes 14680064 | tf_op jit(solution)/shard_map/dot_general | solution.py:157
  478.0 69.2 %all-reduce.10.cloned.1.call-done = f32[1024,1024]{0,1:T(8,128)} async-done(((f32[1024,1024]{0,1:T(8,128)}), f32[1024,1024]{0,1:T(8,128)}) %all-reduce.10.cloned.1.call-update) | async-done | bytes 4194320 | tf_op jit(solution)/shard_map/psum | solution.py:160
  547.2 6.0 multiply_reduce_fusion.3
  576.1 8.3 multiply_convert_fusion
  600.5 153.5 %all-reduce.12.cloned.1.call-done = (f32[1024,1024]{0,1:T(8,128)}, f32[1024,1024]{0,1:T(8,128)}) async-done(((f32[1024,1024]{0,1:T(8,128)}, f32[1024,1024]{0,1:T(8,128)}), (f32[1024,1024]{0,1:T(8,128)}, f32[1024,1024]{0,1:T(8,128)})) %all-reduce.12.cloned.1.call-update) | async-done | bytes 8388624 | tf_op jit(solution)/shard_map/psum | solution.py:152
  754.0 6.0 multiply_reduce_fusion.2
  789.8 6.0 fusion.132
  810.0 10.7 fusion
  831.6 97.4 %reduce-scatter.8.cloned.1.call-done = f32[1000,256]{1,0:T(8,128)} async-done(((f32[8000,256]{1,0:T(8,128)}), f32[1000,256]{1,0:T(8,128)}) %reduce-scatter.8.cloned.1.call-update) | async-done | bytes 1024016 | tf_op jit(solution)/shard_map/reduce_scatter | solution.py:248
  933.1 62.9 %reduce-scatter.16.cloned.1.call-done = f32[256,128]{1,0:T(8,128)} async-done(((f32[256,1024]{1,0:T(8,128)}), f32[256,128]{1,0:T(8,128)}) %reduce-scatter.16.cloned.1.call-update) | async-done | bytes 131088 | tf_op jit(solution)/shard_map/reduce_scatter | solution.py:245
  996.0 66.6 %reduce-scatter.10.cloned.1.call-done = f32[32,1024]{1,0:T(8,128)} async-done(((f32[256,1024]{1,0:T(8,128)}), f32[32,1024]{1,0:T(8,128)}) %reduce-scatter.10.cloned.1.call-update) | async-done | bytes 131088 | tf_op jit(solution)/shard_map/reduce_scatter | solution.py:242
  1062.6 91.5 %reduce-scatter.20.cloned.1.call-done = f32[1024,128]{1,0:T(8,128)} async-done(((f32[1024,1024]{1,0:T(8,128)}), f32[1024,128]{1,0:T(8,128)}) %reduce-scatter.20.cloned.1.call-update) | async-done | bytes 524304 | tf_op jit(solution)/shard_map/reduce_scatter | solution.py:247
  1154.2 92.4 %reduce-scatter.18.cloned.1.call-done = f32[128,1024]{1,0:T(8,128)} async-done(((f32[1024,1024]{1,0:T(8,128)}), f32[128,1024]{1,0:T(8,128)}) %reduce-scatter.18.cloned.1.call-update) | async-done | bytes 524304 | tf_op jit(solution)/shard_map/reduce_scatter | solution.py:246
  1246.5 78.2 %reduce-scatter.14.cloned.1.call-done = f32[128,768]{1,0:T(8,128)} async-done(((f32[1024,768]{1,0:T(8,128)}), f32[128,768]{1,0:T(8,128)}) %reduce-scatter.14.cloned.1.call-update) | async-done | bytes 393232 | tf_op jit(solution)/shard_map/reduce_scatter | solution.py:244
  1324.8 91.2 %reduce-scatter.12.cloned.1.call-done = f32[32,4096]{1,0:T(8,128)} async-done(((f32[256,4096]{1,0:T(8,128)}), f32[32,4096]{1,0:T(8,128)}) %reduce-scatter.12.cloned.1.call-update) | async-done | bytes 524304 | tf_op jit(solution)/shard_map/reduce_scatter | solution.py:243
  (268 shorter events, 189.8 us)
Async XLA Ops:
  7.2 79.5 %all-gather.6.cloned.1.call-start = ((), (), s32[]{:S(2)}) async-start(), calls=%async_computation.7 | async-start | bytes 4608000 | tf_op jit(solution)/shard_map/all_gather | solution.py:82
  11.7 148.2 %all-gather.8.cloned.1.call-start = ((), (), s32[]{:S(2)}) async-start(), calls=%async_computation.9 | async-start | bytes 2359296 | tf_op jit(solution)/shard_map/all_gather | solution.py:67
  12.5 169.7 %all-reduce.6.cloned.1.call-start = ((), (), s32[]{:S(2)}) async-start(), calls=%async_computation.8 | async-start | bytes 1048576 | tf_op jit(solution)/shard_map/psum | solution.py:91
  12.5 80.4 %copy-start.29 = (s32[8000]{0:T(1024)}, s32[8000]{0:T(1024)S(1)}, u32[]{:S(2)}) copy-start(s32[8000]{0:T(1024)S(1)} %fusion.106) | copy-start | bytes 96004
  13.4 78.2 %copy-start.60 = (s32[256]{0:T(256)}, s32[256]{0:T(256)S(1)}, u32[]{:S(2)}) copy-start(s32[256]{0:T(256)S(1)} %get-tuple-element.51) | copy-start | bytes 3076
  13.4 78.2 %copy-start.62 = (s32[256]{0:T(256)}, s32[256]{0:T(256)S(1)}, u32[]{:S(2)}) copy-start(s32[256]{0:T(256)S(1)} %get-tuple-element.49) | copy-start | bytes 3076
  13.4 79.6 %copy-start.56 = (s32[256]{0:T(256)}, s32[256]{0:T(256)S(1)}, u32[]{:S(2)}) copy-start(s32[256]{0:T(256)S(1)} %get-tuple-element.48) | copy-start | bytes 3076
  95.2 133.2 %all-gather.10.cloned.1.call-start = ((), (), s32[]{:S(2)}) async-start(), calls=%async_computation.10 | async-start | bytes 1769472 | tf_op jit(solution)/shard_map/all_gather | solution.py:68
  95.8 243.1 %all-reduce.8.cloned.1.call-start = ((), (), s32[]{:S(2)}) async-start(), calls=%async_computation.11 | async-start | bytes 8388608 | tf_op jit(solution)/shard_map/psum | solution.py:143
  254.5 136.1 %all-gather.12.cloned.1.call-start = ((), (), s32[]{:S(2)}) async-start(), calls=%async_computation.12 | async-start | bytes 2359296 | tf_op jit(solution)/shard_map/all_gather | solution.py:70
  255.0 187.4 %all-gather.14.cloned.1.call-start = ((), (), s32[]{:S(2)}) async-start(), calls=%async_computation.13 | async-start | bytes 2359296 | tf_op jit(solution)/shard_map/all_gather | solution.py:71
  255.8 291.4 %all-reduce.10.cloned.1.call-start = ((), (), s32[]{:S(2)}) async-start(), calls=%async_computation.14 | async-start | bytes 8388608 | tf_op jit(solution)/shard_map/psum | solution.py:160
  463.4 290.7 %all-reduce.12.cloned.1.call-start = ((), (), s32[]{:S(2)}) async-start(), calls=%async_computation.22 | async-start | bytes 16777216 | tf_op jit(solution)/shard_map/psum | solution.py:152
  466.7 92.4 %copy-start.13 = (bf16[1024,1024]{0,1:T(8,128)(2,1)}, bf16[1024,1024]{0,1:T(8,128)(2,1)S(1)}, u32[]{:S(2)}) copy-start(bf16[1024,1024]{0,1:T(8,128)(2,1)S(1)} %copy.68) | copy-start | bytes 6291460
  600.5 328.6 %reduce-scatter.8.cloned.1.call-start = ((), (), s32[]{:S(2)}) async-start(), calls=%async_computation.15 | async-start | bytes 9216000 | tf_op jit(solution)/shard_map/reduce_scatter | solution.py:248
  782.5 213.5 %reduce-scatter.16.cloned.1.call-start = ((), (), s32[]{:S(2)}) async-start(), calls=%async_computation.19 | async-start | bytes 1179648 | tf_op jit(solution)/shard_map/reduce_scatter | solution.py:245
  785.9 276.8 %reduce-scatter.10.cloned.1.call-start = ((), (), s32[]{:S(2)}) async-start(), calls=%async_computation.16 | async-start | bytes 1179648 | tf_op jit(solution)/shard_map/reduce_scatter | solution.py:242
  789.7 364.5 %reduce-scatter.20.cloned.1.call-start = ((), (), s32[]{:S(2)}) async-start(), calls=%async_computation.21 | async-start | bytes 4718592 | tf_op jit(solution)/shard_map/reduce_scatter | solution.py:247
  795.8 450.7 %reduce-scatter.18.cloned.1.call-start = ((), (), s32[]{:S(2)}) async-start(), calls=%async_computation.20 | async-start | bytes 4718592 | tf_op jit(solution)/shard_map/reduce_scatter | solution.py:246
  803.3 521.4 %reduce-scatter.14.cloned.1.call-start = ((), (), s32[]{:S(2)}) async-start(), calls=%async_computation.18 | async-start | bytes 3538944 | tf_op jit(solution)/shard_map/reduce_scatter | solution.py:244
  809.9 606.1 %reduce-scatter.12.cloned.1.call-start = ((), (), s32[]{:S(2)}) async-start(), calls=%async_computation.17 | async-start | bytes 4718592 | tf_op jit(solution)/shard_map/reduce_scatter | solution.py:243
  829.1 100.0 %copy-start.21 = (bf16[1000,256]{1,0:T(8,128)(2,1)S(1)}, bf16[1000,256]{1,0:T(8,128)(2,1)}, u32[]{:S(2)}) copy-start(bf16[1000,256]{1,0:T(8,128)(2,1)} %param.14) | copy-start | bytes 1536004
  829.1 101.5 %copy-start.51 = (f32[1000]{0:T(1024)S(1)}, f32[1000]{0:T(1024)}, u32[]{:S(2)}) copy-start(f32[1000]{0:T(1024)} %copy-done.50) | copy-start | bytes 12004
  829.1 101.5 %copy-start.49 = (f32[1000]{0:T(1024)S(1)}, f32[1000]{0:T(1024)}, u32[]{:S(2)}) copy-start(f32[1000]{0:T(1024)} %copy-done.48) | copy-start | bytes 12004
  (67 other events, 598.8 us)
Sparse Core Ops, SparseCore 0:
  11.8 74.8 all-gather.5
  88.8 52.0 all-gather.7
  143.8 38.2 all-reduce.5
  184.1 44.1 all-gather.9
  254.6 84.2 all-reduce.7
  341.1 49.4 all-gather.11
  392.8 49.5 all-gather.13
  463.5 83.6 all-reduce.9
  600.6 153.3 all-reduce.11
  782.6 146.4 reduce-scatter.7
  933.1 62.8 reduce-scatter.15
  1000.2 62.3 reduce-scatter.9
  1066.8 87.2 reduce-scatter.19
  1158.7 87.8 reduce-scatter.17
  1250.5 74.1 reduce-scatter.13
  1328.8 87.0 reduce-scatter.11
where the time goes:
time: 1430 us; the launch traced here: 1420 us
  waiting for transfers between devices  1090 us (76%)
  matrix products  140 us (10%)
  other arithmetic  76.8 us (5%)
  blocking collectives  62.9 us (4%)
  local copies, waits for them, and re-layouts  32.6 us (2%)
  between operations  15.3 us (1%)
    psum x1, waiting for transfers between devices, per_device(): lax.psum(jnp.dot(activated_low, down_full, preferred_element_type=jnp.flo...  153 us
    reduce_scatter x1, waiting for transfers between devices, per_device(): lax.psum_scatter(grad_normed, 'dp', scatter_dimension=0, tiled=True)  97.4 us
    reduce_scatter x1, waiting for transfers between devices, per_device(): lax.psum_scatter(grad_up, 'dp', scatter_dimension=0, tiled=True)  92.4 us
    reduce_scatter x1, waiting for transfers between devices, per_device(): lax.psum_scatter(grad_down, 'dp', scatter_dimension=1, tiled=True)  91.5 us
    reduce_scatter x1, waiting for transfers between devices, per_device(): lax.psum_scatter(grad_time, 'dp', scatter_dimension=0, tiled=True)  91.2 us
    psum x1, waiting for transfers between devices, per_device(): lax.psum(jnp.dot(attended, output_full, preferred_element_type=jnp.float3...  82.9 us
    reduce_scatter x1, waiting for transfers between devices, per_device(): lax.psum_scatter(grad_project, 'dp', scatter_dimension=0, tiled=True)  78.2 us
    all_gather x1, waiting for transfers between devices, per_device(): piece = lax.all_gather(normed_low, 'dp', axis=0, tiled=True)  73.3 us
  transfers between devices with their start and end apart: 16, of which 15 were waited for; matrix products, arithmetic and copies ran while one was open for 8% of the time, Pallas kernels for 0%

commit v1 on v0

v1 whole, which is shorter than its diff:
```python
import math

import jax
import jax.numpy as jnp
from jax import lax
from jax.sharding import PartitionSpec as P

HD = 64
EMB = 256

table_eps = 1e-06
norm_eps = 1e-05
bf16 = jnp.bfloat16
f32 = jnp.float32


def dot(left, right, dims=((1,), (0,))):
    return lax.dot_general(left, right, (dims, ((), ())), preferred_element_type=f32)


SWAP_CORE = [(0, 1), (1, 0), (2, 3), (3, 2)]
SWAP_X = [(0, 2), (2, 0), (1, 3), (3, 1)]


def swap_core(value):
    return lax.ppermute(value, "tensor", SWAP_CORE)


def swap_x(value):
    return lax.ppermute(value, "tensor", SWAP_X)


class Direct:
    def __init__(self, count):
        self.count, self.chain = count, count // 2
        me = lax.axis_index("dp")
        z, y = me // 2, me % 2
        self.places = [
            ((z - dz) % self.chain) * 2 + (y ^ dy) for dy in range(2) for dz in range(self.chain)
        ]

    def step(self, value, dz, dy):
        pairs = [
            (z * 2 + y, ((z + dz) % self.chain) * 2 + (y ^ dy))
            for z in range(self.chain)
            for y in range(2)
        ]
        return lax.ppermute(value, "dp", pairs)

    def spread(self, value):
        near = [value] + [self.step(value, dz, 0) for dz in range(1, self.chain)]
        return near + [self.step(value, dz, 1) for dz in range(self.chain)]

    def spread_small(self, value):
        both = jnp.stack([value, self.step(value, 0, 1)])
        rings = [both] + [self.step(both, dz, 0) for dz in range(1, self.chain)]
        return [ring[dy] for dy in range(2) for ring in rings]

    def collect(self, values):
        arrived = [values[0]]
        for k in range(1, self.count):
            dy, dz = divmod(k, self.chain)
            arrived.append(self.step(values[k], -dz, dy))
        return arrived

    def gather(self, block, axis):
        near = jnp.concatenate(
            [block] + [self.step(block, dz, 0) for dz in range(1, self.chain)], axis=axis
        )
        return jnp.concatenate([near, self.step(near, 0, 1)], axis=axis)

    def scatter(self, whole, axis):
        near, far = jnp.split(whole, 2, axis=axis)
        near = near + self.step(far.astype(bf16), 0, 1).astype(f32)
        blocks = jnp.split(near, self.chain, axis=axis)
        total = blocks[0]
        for dz in range(1, self.chain):
            total = total + self.step(blocks[dz].astype(bf16), -dz, 0).astype(f32)
        return total


class Plain:
    def __init__(self, count):
        self.count = count
        self.places = list(range(count))

    def spread(self, value):
        return list(lax.all_gather(value, "dp"))

    spread_small = spread

    def collect(self, values):
        stacked = jnp.stack(values).astype(f32)
        return [lax.psum_scatter(stacked, "dp", scatter_dimension=0, tiled=False)]

    def gather(self, block, axis):
        return lax.all_gather(block, "dp", axis=axis, tiled=True)

    def scatter(self, whole, axis):
        return lax.psum_scatter(whole, "dp", scatter_dimension=axis, tiled=True)


def block_order(value, places, axis):
    size = value.shape[axis] // len(places)
    return jnp.concatenate(
        [lax.dynamic_slice_in_dim(value, place * size, size, axis) for place in places], axis=axis
    )


def split_two(value):
    high = value.astype(bf16)
    return high, (value - high.astype(f32)).astype(bf16)


def fold(value, width):
    return jnp.concatenate(jnp.split(value, value.shape[1] // width, axis=1), axis=0)


def unfold(value, count):
    return jnp.concatenate(jnp.split(value, count, axis=0), axis=1)


def norm_parts(value):
    centred = value - jnp.mean(value, axis=-1, keepdims=True)
    inverse = lax.rsqrt(jnp.mean(centred * centred, axis=-1, keepdims=True) + norm_eps)
    return centred * inverse, inverse


def norm_back(grad, normal, inverse, scale):
    inner = grad * (1.0 + scale)
    return inverse * (
        inner
        - jnp.mean(inner, axis=-1, keepdims=True)
        - normal * jnp.mean(inner * normal, axis=-1, keepdims=True)
    )


def per_device(
    token_ids,
    lengths,
    time_steps,
    embed_table,
    input_weight,
    time_weight,
    project_weight,
    output_weight,
    up_weight,
    down_weight,
    cotangent,
):
    rows = token_ids.shape[0]
    half, quarter = rows // 2, rows // 4
    count = lax.axis_size("dp")
    groups = lax.axis_size("tensor")
    me = lax.axis_index("dp")
    place = lax.axis_index("tensor")
    x, c = place // 2, place % 2
    width = cotangent.shape[1]
    docs = lengths.shape[0]
    shard = embed_table.shape[0]
    emb_rows = input_weight.shape[0]
    direct = count % 2 == 0 and count <= 8 and (width // count) % 128 == 0
    dp = Direct(count) if direct else Plain(count)
    places = dp.places
    inverse_places = [
        sum(jnp.where(jnp.int32(places[k]) == a, k, 0) for k in range(count)) for a in range(count)
    ]

    table = embed_table.astype(f32)
    rscale = lax.rsqrt(jnp.mean(table * table, axis=1, keepdims=True) + table_eps)
    normed = (table * rscale).astype(bf16)
    pair = jnp.concatenate([normed, swap_x(normed)], axis=0)
    shards = jnp.concatenate([pair, swap_core(pair)], axis=0)
    owners = [x * 2 + c, (1 - x) * 2 + c, x * 2 + 1 - c, (1 - x) * 2 + 1 - c]
    vocab = jnp.concatenate(
        [(me * groups + owner) * shard + jnp.arange(shard, dtype=jnp.int32) for owner in owners]
    )

    my_ids = lax.dynamic_slice_in_dim(token_ids, (c * 2 + x) * quarter, quarter)
    heard = dp.spread_small(jnp.concatenate([my_ids, time_steps]))
    ids = [message[:quarter] for message in heard]
    steps = jnp.concatenate([message[quarter:] for message in heard])
    feature = me * emb_rows + jnp.arange(emb_rows, dtype=jnp.int32)
    part = EMB // 2
    frequency = jnp.exp(-math.log(10000.0) * (feature % part).astype(f32) / part)
    angles = steps.astype(f32)[:, None] * frequency[None, :]
    features = jnp.where(feature[None, :] < part, jnp.sin(angles), jnp.cos(angles)).astype(bf16)

    packed_one = jnp.concatenate(
        [project_weight, fold(input_weight, EMB), unfold(output_weight, 2)], axis=1
    ) if direct else None
    if direct:
        whole_one = dp.gather(packed_one, 0)
        head_width = project_weight.shape[1]
        project = whole_one[:, :head_width]
        per = width // count
        input_rel = [
            unfold(whole_one[k * per : (k + 1) * per, head_width : head_width + EMB], width // EMB)
            for k in range(count)
        ]
        output = jnp.concatenate(
            [
                fold(whole_one[k * per : (k + 1) * per, head_width + EMB :], per)
                for k in range(count)
            ],
            axis=1,
        )
        input_rows = block_order(jnp.concatenate(input_rel, axis=0), inverse_places, 0)
        input_full = block_order(input_rows, places, 1)
    else:
        project = dp.gather(project_weight, 0)
        input_full = dp.gather(input_weight, 0)
        output = dp.gather(output_weight, 1)
    down = dp.gather(down_weight, 1)
    up = dp.gather(up_weight, 0)

    time_part = lax.dynamic_slice_in_dim(time_weight, place * width, width, 1)
    messages = []
    for k in range(count):
        onehot = (ids[k][:, None] == vocab[None, :]).astype(bf16)
        found = dot(onehot, shards).astype(bf16)
        mods = dot(features[k * docs : (k + 1) * docs], time_part)
        high, low = split_two(mods)
        messages.append(
            jnp.concatenate([found, fold(jnp.concatenate([high, low], axis=0), EMB)], axis=0)
        )
    arrived = sum(message.astype(f32) for message in dp.collect(messages))
    embed_quarter = arrived[:quarter].astype(bf16)
    mods = unfold(arrived[quarter:], width // EMB)
    mods = mods[:docs] + mods[docs:]
    mods = block_order(mods, places, 1)
    high, low = split_two(mods)
    mine = jnp.concatenate(
        [embed_quarter, fold(jnp.concatenate([high, low], axis=0), EMB)], axis=0
    )
    other = swap_x(mine)
    both = jnp.stack([jnp.where(x == 0, mine, other), jnp.where(x == 0, other, mine)])
    far = swap_core(both)
    embed = jnp.concatenate(
        [both[0, :quarter], far[0, :quarter], both[1, :quarter], far[1, :quarter]], axis=0
    )
    blocks = []
    for at in range(2):
        first = jnp.where(c == 0, both[at, quarter:], far[at, quarter:])
        second = jnp.where(c == 0, far[at, quarter:], both[at, quarter:])
        blocks += [unfold(first, width // EMB), unfold(second, width // EMB)]
    position = jnp.concatenate(
        [
            start + jnp.arange(quarter, dtype=jnp.int32)
            for start in (c * half, (1 - c) * half, c * half + quarter, (1 - c) * half + quarter)
        ]
    )
    ends = jnp.cumsum(lengths)
    document = jnp.sum((position[:, None] >= ends[None, :]).astype(jnp.int32), axis=1)
    member = document[:, None] == jnp.arange(docs, dtype=jnp.int32)[None, :]
    member = member.astype(bf16)
    member_two = jnp.concatenate([member, member], axis=1)

    def own(value):
        return jnp.concatenate([value[:quarter], value[half : half + quarter]], axis=0)

    member_own = own(member)
    member_two_own = own(member_two)

    stream_zero = dot(embed, input_full)
    normal_one, inverse_one = norm_parts(stream_zero)
    scale_one = dot(member_two, blocks[0])
    hidden_one = (normal_one * (1.0 + scale_one) + dot(member_two, blocks[1])).astype(bf16)
    stream_zero = own(stream_zero)
    normal_one, inverse_one = norm_parts(stream_zero)

    projected = dot(hidden_one, project).astype(bf16)
    heads = projected.shape[1] // (3 * HD)
    split = projected.reshape(rows, heads, 3, HD)
    query = jnp.transpose(split[:, :, 0], (1, 0, 2)) * jnp.asarray(1.0 / math.sqrt(HD), bf16)
    keys = jnp.transpose(split[:, :, 1], (1, 0, 2))
    values = jnp.transpose(split[:, :, 2], (1, 0, 2))
    same = (document[:, None] == document[None, :])[None]

    def batched(left, right, spec):
        return jnp.einsum(spec, left, right, preferred_element_type=f32)

    scores = jnp.where(same, batched(query, keys, "hqd,hkd->hqk"), -1e30)
    peak = jnp.max(scores, axis=2, keepdims=True)
    expo = jnp.exp(scores - peak)
    total = jnp.sum(expo, axis=2, keepdims=True)
    probs = (expo / total).astype(bf16)
    attended = (
        jnp.transpose(batched(probs, values, "hqk,hkd->hqd"), (1, 0, 2))
        .reshape(rows, heads * HD)
        .astype(bf16)
    )

    def reduce_chunk(partial):
        mine = partial[:quarter] + swap_core(partial[quarter:].astype(bf16)).astype(f32)
        mine = mine.astype(bf16)
        return mine.astype(f32) + swap_x(mine).astype(f32)

    cot = cotangent.reshape(4, quarter, width)
    cot = jnp.where(
        c == 0,
        jnp.concatenate([cot[0], cot[2], cot[1], cot[3]], axis=0),
        jnp.concatenate([cot[2], cot[0], cot[3], cot[1]], axis=0),
    )
    if direct:
        cot = block_order(cot, places, 1)
    attention = [
        reduce_chunk(dot(attended[at * half : (at + 1) * half], output)) for at in range(2)
    ]
    stream_one, normals, inverses, scales, hidden_two = [], [], [], [], []
    for at in range(2):
        stream = stream_zero[at * quarter : (at + 1) * quarter] + attention[at]
        normal, inverse = norm_parts(stream)
        members = member_two_own[at * quarter : (at + 1) * quarter]
        scale = dot(members, blocks[2])
        hidden = (normal * (1.0 + scale) + dot(members, blocks[3])).astype(bf16)
        hidden_two.append(jnp.concatenate([hidden, swap_core(hidden)], axis=0))
        stream_one.append(stream)
        normals.append(normal)
        inverses.append(inverse)
        scales.append(scale)
    activated, grad_upward, grad_two, branch = [], [], [], []
    for at in range(2):
        upward = dot(hidden_two[at], up)
        phi = 0.5 * (1.0 + lax.erf(upward * math.sqrt(0.5)))
        active = (upward * phi).astype(bf16)
        slope = phi + upward * (math.sqrt(0.5 / math.pi) * jnp.exp(-0.5 * upward * upward))
        grad_active = dot(cot[at * half : (at + 1) * half], down, ((1,), (1,)))
        grad_up_rows = (grad_active * slope).astype(bf16)
        activated.append(active)
        grad_upward.append(grad_up_rows)
        grad_two.append(reduce_chunk(dot(grad_up_rows, up, ((1,), (1,)))))
    for at in range(2):
        branch.append(reduce_chunk(dot(activated[at], down)))
    activated = jnp.concatenate(activated, axis=0)
    grad_upward = jnp.concatenate(grad_upward, axis=0)
    hidden_two = jnp.concatenate(hidden_two, axis=0)
    grad_down = dot(activated, cot, ((0,), (0,)))
    grad_up = dot(hidden_two, grad_upward, ((0,), (0,)))
    summed_down = dp.scatter(grad_down, 1)
    summed_up = dp.scatter(grad_up, 0)

    out_blocks = []
    for at in range(2):
        block = (stream_one[at] + branch[at]).astype(bf16)
        out_blocks += [block, swap_core(block)]
    block_out = jnp.where(
        c == 0,
        jnp.concatenate([out_blocks[b] for b in (0, 2, 1, 3)], axis=0),
        jnp.concatenate([out_blocks[b] for b in (1, 3, 0, 2)], axis=0),
    )
    if direct:
        block_out = block_order(block_out, inverse_places, 1)

    grad_one, grad_attn, grad_scale_two, grad_shift_two = [], [], 0.0, 0.0
    for at in range(2):
        grad = grad_two[at]
        back = norm_back(grad, normals[at], inverses[at], scales[at])
        stream = cot[at * half : at * half + quarter].astype(f32) + back
        low = stream.astype(bf16)
        grad_attn += [low, swap_core(low)]
        grad_one.append(stream)
        members = member_own[at * quarter : (at + 1) * quarter]
        grad_scale_two += dot(members, (grad * normals[at]).astype(bf16), ((0,), (0,)))
        grad_shift_two += dot(members, grad.astype(bf16), ((0,), (0,)))
    grad_attn = jnp.concatenate(grad_attn, axis=0)
    grad_output = dot(attended, grad_attn, ((0,), (0,)))
    grad_attended = dot(grad_attn, output, ((1,), (1,))).astype(bf16)
    grad_heads = jnp.transpose(grad_attended.reshape(rows, heads, HD), (1, 0, 2))
    attended_heads = jnp.transpose(attended.reshape(rows, heads, HD), (1, 0, 2))
    inner = jnp.sum(
        grad_heads.astype(f32) * attended_heads.astype(f32), axis=2, keepdims=True
    )
    grad_probs = batched(grad_heads, values, "hqd,hkd->hqk")
    grad_scores = (probs.astype(f32) * (grad_probs - inner)).astype(bf16)
    grad_query = batched(grad_scores, keys, "hqk,hkd->hqd") * (1.0 / math.sqrt(HD))
    grad_keys = batched(grad_scores, query, "hqk,hqd->hkd")
    grad_values = batched(probs, grad_heads, "hqk,hqd->hkd")
    grad_projected = (
        jnp.transpose(jnp.stack([grad_query, grad_keys, grad_values], axis=2), (1, 0, 2, 3))
        .reshape(rows, heads * 3 * HD)
        .astype(bf16)
    )
    grad_hidden_one = [
        reduce_chunk(dot(grad_projected[at * half : (at + 1) * half], project, ((1,), (1,))))
        for at in range(2)
    ]
    grad_project = dot(hidden_one, grad_projected, ((0,), (0,)))
    if direct:
        per = width // count
        grad_output = jnp.concatenate(
            [unfold(grad_output[:, k * per : (k + 1) * per], 2) for k in range(count)], axis=0
        )
        summed_one = dp.scatter(jnp.concatenate([grad_project, grad_output], axis=1), 0)
        summed_project = summed_one[:, : grad_project.shape[1]]
        summed_output = fold(summed_one[:, grad_project.shape[1] :], per)
    else:
        summed_project = dp.scatter(grad_project, 0)
        summed_output = dp.scatter(grad_output, 1)

    grad = jnp.concatenate(grad_hidden_one, axis=0)
    back = norm_back(grad, normal_one, inverse_one, own(scale_one))
    grad_zero = (back + jnp.concatenate(grad_one, axis=0)).astype(bf16)
    grad_scale_one = dot(member_own, (grad * normal_one).astype(bf16), ((0,), (0,)))
    grad_shift_one = dot(member_own, grad.astype(bf16), ((0,), (0,)))
    grad_embed = dot(grad_zero, input_full, ((1,), (1,))).astype(bf16)
    grad_embed = jnp.where(x == 0, grad_embed[:quarter], grad_embed[quarter:])
    grad_mods = jnp.concatenate(
        [grad_scale_one, grad_shift_one, grad_scale_two, grad_shift_two], axis=0
    )
    grad_mods = block_order(grad_mods, inverse_places, 1)
    grad_mods = grad_mods + swap_core(grad_mods)
    mod_part = lax.dynamic_slice_in_dim(grad_mods, place * docs, docs, 0).astype(bf16)
    grad_input = dot(own(embed), grad_zero, ((0,), (0,)))
    grad_input = block_order(grad_input, inverse_places, 1)
    columns = width // groups
    mine = lax.dynamic_slice_in_dim(grad_input, place * columns, columns, 1)
    partner = lax.dynamic_slice_in_dim(grad_input, (x * 2 + 1 - c) * columns, columns, 1)
    mine = (mine + swap_core(partner.astype(bf16)).astype(f32)).astype(bf16)
    for_places = [lax.dynamic_slice_in_dim(mine, p * emb_rows, emb_rows, 0) for p in places]
    to_all = jnp.concatenate([grad_embed, fold(mod_part, EMB)], axis=0)
    if direct:
        arrived = []
        for k in range(count):
            dy, dz = divmod(k, dp.chain)
            message = jnp.concatenate([to_all, for_places[(-dz) % dp.chain + dy * dp.chain]], axis=0)
            arrived.append(message if k == 0 else dp.step(message, dz, dy))
        extra = arrived[0].shape[0] - emb_rows
        input_part = sum(message[extra:].astype(f32) for message in arrived)
    else:
        arrived = dp.spread(to_all)
        input_part = dp.collect([block.astype(f32) for block in for_places])[0]
        extra = to_all.shape[0]
    grad_tokens = jnp.concatenate([message[:quarter] for message in arrived], axis=0)
    all_mods = jnp.concatenate(
        [unfold(message[quarter:extra], width // EMB) for message in arrived], axis=0
    )
    time_grad = dot(features, all_mods, ((0,), (0,)))
    small = jnp.concatenate([time_grad, input_part], axis=1)
    other = swap_x(small)
    both = jnp.stack([jnp.where(x == 0, small, other), jnp.where(x == 0, other, small)])
    far = swap_core(both)
    pieces = []
    for at in range(2):
        pieces += [jnp.where(c == 0, both[at], far[at]), jnp.where(c == 0, far[at], both[at])]
    summed_time = jnp.concatenate([piece[:, :width] for piece in pieces], axis=1)
    summed_input = jnp.concatenate([piece[:, width:] for piece in pieces], axis=1)

    all_ids = jnp.concatenate(ids)

    def table_part(at):
        names = vocab[at * 2 * shard : (at + 1) * 2 * shard]
        onehot = (names[:, None] == all_ids[None, :]).astype(bf16)
        return dot(onehot, grad_tokens)

    far = swap_core(table_part(1).astype(bf16))
    near = table_part(0) + far.astype(f32)
    grad_normed = near[:shard] + swap_x(near[shard:].astype(bf16)).astype(f32)
    grad_table = rscale * grad_normed - table * (
        rscale * rscale * rscale * jnp.mean(grad_normed * table, axis=1, keepdims=True)
    )
    return (
        block_out,
        grad_table,
        summed_input,
        summed_time,
        summed_project,
        summed_output,
        summed_up,
        summed_down,
    )


def solution(mesh):
    return jax.shard_map(
        per_device,
        mesh=mesh,
        in_specs=(
            P("dp"),
            P("dp"),
            P("dp"),
            P(("dp", "tensor"), None),
            P("dp", None),
            P("dp", None),
            P("dp", "tensor"),
            P("tensor", "dp"),
            P("dp", "tensor"),
            P("tensor", "dp"),
            P("dp", None),
        ),
        out_specs=(
            P("dp", None),
            P(("dp", "tensor"), None),
            P("dp", None),
            P("dp", None),
            P("dp", "tensor"),
            P("tensor", "dp"),
            P("dp", "tensor"),
            P("tensor", "dp"),
        ),
        check_vma=False,
    )
```

time: 1430 us -> 570 us (0.40)
  waiting for transfers between devices: 1090 us -> 215 us
  starting transfers between devices: 1.52 us -> 114 us
  blocking collectives: 62.9 us -> 0 us
  matrix products: 140 us -> 81.4 us
  local copies, waits for them, and re-layouts: 32.6 us -> 71.2 us
    reduce_scatter x7 -> x0, waiting for transfers between devices: 580 us -> none  [the longest x1 97.4 us: per_device(): lax.psum_scatter(grad_normed, 'dp', scatter_dimension=0, tiled=True)]
    psum x4 -> x0, waiting for transfers between devices: 315 us -> none  [the longest x1 153 us: per_device(): lax.psum(jnp.dot(activated_low, down_full, preferred_element_type=jnp.flo...]
    ppermute x0 -> x74, waiting for transfers between devices: none -> 215 us  [the longest x42 113 us: step(): return lax.ppermute(value, 'dp', pairs)]
    all_gather x5 -> x0, waiting for transfers between devices: 197 us -> none  [the longest x1 73.3 us: per_device(): piece = lax.all_gather(normed_low, 'dp', axis=0, tiled=True)]
    ppermute x0 -> x74, starting transfers between devices: none -> 114 us  [the longest x42 93.2 us: step(): return lax.ppermute(value, 'dp', pairs)]
    all_gather x2 -> x0, blocking collectives: 62.9 us -> none  [the longest x1 32.8 us: per_device(): lax.all_gather(input_weight, 'dp', axis=0, tiled=True)]
    dot_general x39 -> x58, matrix products: 140 us -> 81.4 us  [the longest x52 56.3 us: dot(): lax.dot_general(left, right, (dims, ((), ())), preferred_element_type=f32)]
    reduce_sum x11, other arithmetic: 35.2 us -> 6.07 us  [the longest x3 3.47 us: norm_back(): jnp.mean(inner, axis=-1, keepdims=True)]
  transfers between devices with their start and end apart: 16 -> 74, of which waited for: 15 -> 29; matrix products, arithmetic and copies ran while one was open for 8% -> 27% of each run, Pallas kernels for 0% -> 0%
where the time goes in v1:
time: 570 us; the launch traced here: 561 us
  waiting for transfers between devices  215 us (38%)
  starting transfers between devices  114 us (20%)
  matrix products  81.4 us (14%)
  other arithmetic  75.1 us (13%)
  local copies, waits for them, and re-layouts  71.2 us (12%)
    ppermute x42, waiting for transfers between devices, step(): return lax.ppermute(value, 'dp', pairs)  113 us
    ppermute x12, waiting for transfers between devices, swap_x(): return lax.ppermute(value, 'tensor', SWAP_X)  99.3 us
    ppermute x42, starting transfers between devices, step(): return lax.ppermute(value, 'dp', pairs)  93.2 us
    dot_general x52, matrix products, dot(): lax.dot_general(left, right, (dims, ((), ())), preferred_element_type=f32)  56.3 us
    unnamed x268, local copies, waits for them, and re-layouts  34.3 us
    dot_general x6, matrix products, batched(): return jnp.einsum(spec, left, right, preferred_element_type=f32)  25.1 us
    sub x1, other arithmetic, per_device(): expo = jnp.exp(scores - peak)  18.3 us
    concatenate x7, local copies, waits for them, and re-layouts, per_device(): jnp.concatenate([to_all, for_places[-dz % dp.chain + dy * dp.chain]], axi...  17.5 us
  transfers between devices with their start and end apart: 74, of which 29 were waited for; matrix products, arithmetic and copies ran while one was open for 27% of the time, Pallas kernels for 0%

profile of v1, /device:TPU:0, one launch (start us, length us, event | category | flops | bytes accessed | tf_op | source)
XLA Modules:
  0.0 560.7 jit_solution(5979272529466972169)
XLA Ops:
  41.6 6.1 %collective-permute-start.4 = (s32[2,260]{1,0:T(2,128)S(1)}, s32[2,260]{1,0:T(2,128)S(1)}, u32[]{:S(2)}, u32[]{:S(2)}) collective-permute-start(s32[2,260]{1,0:T(2,128)S(1)} %pad_add_fusion.3), channel_id=1, source_target_pairs={{0,16},{4,20},{8,24},{12,28},{16,0},{20,4},{24,8},{28,12},{1,17},{... | collective-permute-start | bytes 6248 | tf_op jit(solution)/shard_map/ppermute | solution.py:48
  69.6 5.9 %collective-permute-start.28 = (bf16[1024,128]{1,0:T(8,128)(2,1)S(1)}, bf16[1024,128]{1,0:T(8,128)(2,1)S(1)}, u32[]{:S(2)}, u32[]{:S(2)}) collective-permute-start(bf16[1024,128]{1,0:T(8,128)(2,1)S(1)} %copy-done.24), channel_id=1, source_target_pairs={{0,24},{4,28},{8,0},{12,4},{16,8},{20,12},{24,16},{28,20},{1,25},{... | collective-permute-start | bytes 786440 | tf_op jit(solution)/shard_map/ppermute | solution.py:48
  76.8 11.2 %collective-permute-done.27 = bf16[1024,128]{1,0:T(8,128)(2,1)S(1)} collective-permute-done((bf16[1024,128]{1,0:T(8,128)(2,1)S(1)}, bf16[1024,128]{1,0:T(8,128)(2,1)S(1)}, u32[]{:S(2)}, u32[]{:S(2)}) %collective-permute-start.27) | collective-permute-done | bytes 262176 | tf_op jit(solution)/shard_map/ppermute | solution.py:48
  103.1 14.6 %collective-permute-done.25 = bf16[512,1024]{1,0:T(8,128)(2,1)S(1)} collective-permute-done((bf16[512,1024]{1,0:T(8,128)(2,1)S(1)}, bf16[512,1024]{1,0:T(8,128)(2,1)S(1)}, u32[]{:S(2)}, u32[]{:S(2)}) %collective-permute-start.25) | collective-permute-done | bytes 1048608 | tf_op jit(solution)/shard_map/ppermute | solution.py:48
  117.8 22.4 %collective-permute-done.29 = bf16[1024,512]{1,0:T(8,128)(2,1)S(1)} collective-permute-done((bf16[1024,512]{1,0:T(8,128)(2,1)S(1)}, bf16[1024,512]{1,0:T(8,128)(2,1)S(1)}, u32[]{:S(2)}, u32[]{:S(2)}) %collective-permute-start.29) | collective-permute-done | bytes 1048608 | tf_op jit(solution)/shard_map/ppermute | solution.py:48
  155.5 9.8 %collective-permute-done.18 = bf16[512,1280]{1,0:T(8,128)(2,1)S(1)} collective-permute-done((bf16[512,1280]{1,0:T(8,128)(2,1)S(1)}, bf16[512,1280]{1,0:T(8,128)(2,1)S(1)}, u32[]{:S(2)}, u32[]{:S(2)}) %collective-permute-start.18) | collective-permute-done | bytes 1310752 | tf_op jit(solution)/shard_map/ppermute | solution.py:48
  195.1 8.2 %fusion.196 = f32[4,1024,1024]{1,2,0:T(8,128)} fusion(bf16[1024,4,3,64]{0,3,2,1:T(8,128)(2,1)S(1)} %bitcast.166), kind=kOutput, calls=%fused_computation.253 | convolution fusion | flops 537133056 | bytes 17825792 | tf_op jit(solution)/shard_map/hqd,hkd->hqk/dot_general | solution.py:281
  203.3 18.3 %fusion.350 = (f32[4,1024]{1,0:T(4,128)S(1)}, f32[4,1024,1024]{1,2,0:T(8,128)}) fusion(f32[4,1024,1024]{1,2,0:T(8,128)} %fusion.196, pred[1024,1024]{0,1:T(8,128)(4,1)S(1)} %broadcast_compare_fusion), kind=kOutput, calls=%fused_computation.751 | output fusion | flops 16778240 | bytes 34619392 | tf_op jit(solution)/shard_map/sub | solution.py:285
  221.7 15.5 %divide_convert_fusion = bf16[4,1024,1024]{1,2,0:T(8,128)(2,1)S(1)} fusion(f32[4,1024,1024]{1,2,0:T(8,128)} %get-tuple-element.275, f32[4,1024]{1,0:T(4,128)S(1)} %get-tuple-element.274), kind=kLoop, calls=%fused_computation.2 | loop fusion | flops 8388608 | bytes 25182208 | tf_op jit(solution)/shard_map/convert_element_type | solution.py:287
  245.9 10.4 %collective-permute-done.33 = bf16[256,1024]{1,0:T(8,128)(2,1)S(1)} collective-permute-done((bf16[256,1024]{1,0:T(8,128)(2,1)S(1)}, bf16[256,1024]{1,0:T(8,128)(2,1)S(1)}, u32[]{:S(2)}, u32[]{:S(2)}) %collective-permute-start.33) | collective-permute-done | bytes 524320 | tf_op jit(solution)/shard_map/ppermute | solution.py:30
  256.3 10.7 %collective-permute-done.20 = bf16[256,1024]{1,0:T(8,128)(2,1)S(1)} collective-permute-done((bf16[256,1024]{1,0:T(8,128)(2,1)S(1)}, bf16[256,1024]{1,0:T(8,128)(2,1)S(1)}, u32[]{:S(2)}, u32[]{:S(2)}) %collective-permute-start.20) | collective-permute-done | bytes 524320 | tf_op jit(solution)/shard_map/ppermute | solution.py:30
  301.6 10.8 %collective-permute-done.31 = bf16[256,1024]{1,0:T(8,128)(2,1)S(1)} collective-permute-done((bf16[256,1024]{1,0:T(8,128)(2,1)S(1)}, bf16[256,1024]{1,0:T(8,128)(2,1)S(1)}, u32[]{:S(2)}, u32[]{:S(2)}) %collective-permute-start.31) | collective-permute-done | bytes 524320 | tf_op jit(solution)/shard_map/ppermute | solution.py:30
  313.7 10.0 %collective-permute-done.40 = bf16[256,1024]{1,0:T(8,128)(2,1)S(1)} collective-permute-done((bf16[256,1024]{1,0:T(8,128)(2,1)S(1)}, bf16[256,1024]{1,0:T(8,128)(2,1)S(1)}, u32[]{:S(2)}, u32[]{:S(2)}) %collective-permute-start.40) | collective-permute-done | bytes 524320 | tf_op jit(solution)/shard_map/ppermute | solution.py:30
  325.0 9.9 %collective-permute-done.36 = bf16[256,1024]{1,0:T(8,128)(2,1)S(1)} collective-permute-done((bf16[256,1024]{1,0:T(8,128)(2,1)S(1)}, bf16[256,1024]{1,0:T(8,128)(2,1)S(1)}, u32[]{:S(2)}, u32[]{:S(2)}) %collective-permute-start.36) | collective-permute-done | bytes 524320 | tf_op jit(solution)/shard_map/ppermute | solution.py:30
  334.9 10.3 %collective-permute-done.43 = bf16[256,1024]{1,0:T(8,128)(2,1)S(1)} collective-permute-done((bf16[256,1024]{1,0:T(8,128)(2,1)S(1)}, bf16[256,1024]{1,0:T(8,128)(2,1)S(1)}, u32[]{:S(2)}, u32[]{:S(2)}) %collective-permute-start.43) | collective-permute-done | bytes 524320 | tf_op jit(solution)/shard_map/ppermute | solution.py:30
  358.8 6.2 %collective-permute-done.71 = bf16[1024,128]{1,0:T(8,128)(2,1)S(1)} collective-permute-done((bf16[1024,128]{1,0:T(8,128)(2,1)S(1)}, bf16[1024,128]{1,0:T(8,128)(2,1)S(1)}, u32[]{:S(2)}, u32[]{:S(2)}) %collective-permute-start.71) | collective-permute-done | bytes 262176 | tf_op jit(solution)/shard_map/ppermute | solution.py:48
  366.7 14.4 %collective-permute-done.72 = bf16[1024,128]{1,0:T(8,128)(2,1)S(1)} collective-permute-done((bf16[1024,128]{1,0:T(8,128)(2,1)S(1)}, bf16[1024,128]{1,0:T(8,128)(2,1)S(1)}, u32[]{:S(2)}, u32[]{:S(2)}) %collective-permute-start.72) | collective-permute-done | bytes 262176 | tf_op jit(solution)/shard_map/ppermute | solution.py:48
  381.1 10.4 %collective-permute-start.69 = (bf16[128,1024]{1,0:T(8,128)(2,1)S(1)}, bf16[128,1024]{1,0:T(8,128)(2,1)S(1)}, u32[]{:S(2)}, u32[]{:S(2)}) collective-permute-start(bf16[128,1024]{1,0:T(8,128)(2,1)S(1)} %get-tuple-element.124), channel_id=1, source_target_pairs={{0,8},{4,12},{8,16},{12,20},{16,24},{20,28},{24,0},{28,4},{1,9},{5... | collective-permute-start | bytes 786440 | tf_op jit(solution)/shard_map/ppermute | solution.py:48
  392.4 9.8 %collective-permute-done.68 = bf16[128,1024]{1,0:T(8,128)(2,1)S(1)} collective-permute-done((bf16[128,1024]{1,0:T(8,128)(2,1)S(1)}, bf16[128,1024]{1,0:T(8,128)(2,1)S(1)}, u32[]{:S(2)}, u32[]{:S(2)}) %collective-permute-start.68) | collective-permute-done | bytes 262176 | tf_op jit(solution)/shard_map/ppermute | solution.py:48
  436.2 12.1 %collective-permute-done.46 = bf16[256,1024]{1,0:T(8,128)(2,1)S(1)} collective-permute-done((bf16[256,1024]{1,0:T(8,128)(2,1)S(1)}, bf16[256,1024]{1,0:T(8,128)(2,1)S(1)}, u32[]{:S(2)}, u32[]{:S(2)}) %collective-permute-start.46) | collective-permute-done | bytes 524320 | tf_op jit(solution)/shard_map/ppermute | solution.py:30
  448.4 10.6 %collective-permute-done.48 = bf16[256,1024]{1,0:T(8,128)(2,1)S(1)} collective-permute-done((bf16[256,1024]{1,0:T(8,128)(2,1)S(1)}, bf16[256,1024]{1,0:T(8,128)(2,1)S(1)}, u32[]{:S(2)}, u32[]{:S(2)}) %collective-permute-start.48) | collective-permute-done | bytes 524320 | tf_op jit(solution)/shard_map/ppermute | solution.py:30
  501.1 8.4 %collective-permute-start.52 = (bf16[304,256]{1,0:T(8,128)(2,1)S(1)}, bf16[304,256]{1,0:T(8,128)(2,1)S(1)}, u32[]{:S(2)}, u32[]{:S(2)}) collective-permute-start(bf16[304,256]{1,0:T(8,128)(2,1)S(1)} %copy-done.40), channel_id=1, source_target_pairs={{0,16},{4,20},{8,24},{12,28},{16,0},{20,4},{24,8},{28,12},{1,17},{... | collective-permute-start | bytes 466952 | tf_op jit(solution)/shard_map/ppermute | solution.py:48
  512.8 7.8 %collective-permute-done.52 = bf16[304,256]{1,0:T(8,128)(2,1)S(1)} collective-permute-done((bf16[304,256]{1,0:T(8,128)(2,1)S(1)}, bf16[304,256]{1,0:T(8,128)(2,1)S(1)}, u32[]{:S(2)}, u32[]{:S(2)}) %collective-permute-start.52) | collective-permute-done | bytes 155680 | tf_op jit(solution)/shard_map/ppermute | solution.py:48
  547.3 11.4 %collective-permute-done.59 = bf16[1000,256]{1,0:T(8,128)(2,1)S(1)} collective-permute-done((bf16[1000,256]{1,0:T(8,128)(2,1)S(1)}, bf16[1000,256]{1,0:T(8,128)(2,1)S(1)}, u32[]{:S(2)}, u32[]{:S(2)}) %collective-permute-start.59) | collective-permute-done | bytes 512032 | tf_op jit(solution)/shard_map/ppermute | solution.py:30
  (702 shorter events, 291.4 us)
Async XLA Ops:
  4.2 89.2 %collective-permute-start.15 = (bf16[128,1280]{1,0:T(8,128)(2,1)}, bf16[128,1280]{1,0:T(8,128)(2,1)}, u32[]{:S(2)}, u32[]{:S(2)}) collective-permute-start(bf16[128,1280]{1,0:T(8,128)(2,1)} %get-tuple-element.170), channel_id=1, source_target_pairs={{0,8},{4,12},{8,16},{12,20},{16,24},{20,28},{24,0},{28,4},{1,9},{5... | collective-permute-start | bytes 983048 | tf_op jit(solution)/shard_map/ppermute | solution.py:48
  7.2 86.7 %collective-permute-start.16 = (bf16[128,1280]{1,0:T(8,128)(2,1)}, bf16[128,1280]{1,0:T(8,128)(2,1)}, u32[]{:S(2)}, u32[]{:S(2)}) collective-permute-start(bf16[128,1280]{1,0:T(8,128)(2,1)} %get-tuple-element.170), channel_id=1, source_target_pairs={{0,16},{4,20},{8,24},{12,28},{16,0},{20,4},{24,8},{28,12},{1,17},{... | collective-permute-start | bytes 983048 | tf_op jit(solution)/shard_map/ppermute | solution.py:48
  9.8 48.6 %collective-permute-start.22 = (bf16[128,1024]{1,0:T(8,128)(2,1)}, bf16[128,1024]{1,0:T(8,128)(2,1)}, u32[]{:S(2)}, u32[]{:S(2)}) collective-permute-start(bf16[128,1024]{1,0:T(8,128)(2,1)} %param.19), channel_id=1, source_target_pairs={{0,8},{4,12},{8,16},{12,20},{16,24},{20,28},{24,0},{28,4},{1,9},{5... | collective-permute-start | bytes 786440 | tf_op jit(solution)/shard_map/ppermute | solution.py:48
  9.8 51.0 %collective-permute-start.23 = (bf16[128,1024]{1,0:T(8,128)(2,1)}, bf16[128,1024]{1,0:T(8,128)(2,1)}, u32[]{:S(2)}, u32[]{:S(2)}) collective-permute-start(bf16[128,1024]{1,0:T(8,128)(2,1)} %param.19), channel_id=1, source_target_pairs={{0,16},{4,20},{8,24},{12,28},{16,0},{20,4},{24,8},{28,12},{1,17},{... | collective-permute-start | bytes 786440 | tf_op jit(solution)/shard_map/ppermute | solution.py:48
  60.8 33.2 %collective-permute-start.17 = (bf16[128,1280]{1,0:T(8,128)(2,1)}, bf16[128,1280]{1,0:T(8,128)(2,1)S(1)}, u32[]{:S(2)}, u32[]{:S(2)}) collective-permute-start(bf16[128,1280]{1,0:T(8,128)(2,1)} %get-tuple-element.170), channel_id=1, source_target_pairs={{0,24},{4,28},{8,0},{12,4},{16,8},{20,12},{24,16},{28,20},{1,25},{... | collective-permute-start | bytes 983048 | tf_op jit(solution)/shard_map/ppermute | solution.py:48
  91.6 26.1 %collective-permute-start.25 = (bf16[512,1024]{1,0:T(8,128)(2,1)S(1)}, bf16[512,1024]{1,0:T(8,128)(2,1)S(1)}, u32[]{:S(2)}, u32[]{:S(2)}) collective-permute-start(bf16[512,1024]{1,0:T(8,128)(2,1)S(1)} %pad_maximum_fusion.6), channel_id=1, source_target_pairs={{0,4},{4,0},{8,12},{12,8},{16,20},{20,16},{24,28},{28,24},{1,5},{5... | collective-permute-start | bytes 3145736 | tf_op jit(solution)/shard_map/ppermute | solution.py:48
  93.4 46.8 %collective-permute-start.29 = (bf16[1024,512]{1,0:T(8,128)(2,1)S(1)}, bf16[1024,512]{1,0:T(8,128)(2,1)S(1)}, u32[]{:S(2)}, u32[]{:S(2)}) collective-permute-start(bf16[1024,512]{1,0:T(8,128)(2,1)S(1)} %pad_maximum_fusion.7), channel_id=1, source_target_pairs={{0,4},{4,0},{8,12},{12,8},{16,20},{20,16},{24,28},{28,24},{1,5},{5... | collective-permute-start | bytes 3145736 | tf_op jit(solution)/shard_map/ppermute | solution.py:48
  95.9 69.4 %collective-permute-start.18 = (bf16[512,1280]{1,0:T(8,128)(2,1)S(1)}, bf16[512,1280]{1,0:T(8,128)(2,1)S(1)}, u32[]{:S(2)}, u32[]{:S(2)}) collective-permute-start(bf16[512,1280]{1,0:T(8,128)(2,1)S(1)} %pad_maximum_fusion.5), channel_id=1, source_target_pairs={{0,4},{4,0},{8,12},{12,8},{16,20},{20,16},{24,28},{28,24},{1,5},{5... | collective-permute-start | bytes 3932168 | tf_op jit(solution)/shard_map/ppermute | solution.py:48
  100.8 39.5 %collective-permute-start.1 = (bf16[2000,256]{1,0:T(8,128)(2,1)S(1)}, bf16[2000,256]{1,0:T(8,128)(2,1)S(1)}, u32[]{:S(2)}, u32[]{:S(2)}) collective-permute-start(bf16[2000,256]{1,0:T(8,128)(2,1)S(1)} %pad_maximum_fusion.8), channel_id=1, source_target_pairs={{0,1},{1,0},{2,3},{3,2},{4,5},{5,4},{6,7},{7,6},{8,9},{9,8},{10,11... | collective-permute-start | bytes 3072008 | tf_op jit(solution)/shard_map/ppermute | solution.py:26
  142.5 29.1 %collective-permute-start.6 = (bf16[288,256]{1,0:T(8,128)(2,1)S(1)}, bf16[288,256]{1,0:T(8,128)(2,1)S(1)}, u32[]{:S(2)}, u32[]{:S(2)}) collective-permute-start(bf16[288,256]{1,0:T(8,128)(2,1)S(1)} %constant_dynamic-update-slice_fusion.4), channel_id=1, source_target_pairs={{0,24},{4,28},{8,0},{12,4},{16,8},{20,12},{24,16},{28,20},{1,25},{... | collective-permute-start | bytes 442376 | tf_op jit(solution)/shard_map/ppermute | solution.py:48
  280.8 72.9 %collective-permute-start.70 = (bf16[1024,512]{1,0:T(8,128)(2,1)S(1)}, bf16[1024,512]{1,0:T(8,128)(2,1)}, u32[]{:S(2)}, u32[]{:S(2)}) collective-permute-start(bf16[1024,512]{1,0:T(8,128)(2,1)S(1)} %split.1191), channel_id=1, source_target_pairs={{0,4},{4,0},{8,12},{12,8},{16,20},{20,16},{24,28},{28,24},{1,5},{5... | collective-permute-start | bytes 3145736 | tf_op jit(solution)/shard_map/ppermute | solution.py:48
  293.8 62.8 %collective-permute-start.66 = (bf16[512,1024]{1,0:T(8,128)(2,1)S(1)}, bf16[512,1024]{1,0:T(8,128)(2,1)S(1)}, u32[]{:S(2)}, u32[]{:S(2)}) collective-permute-start(bf16[512,1024]{1,0:T(8,128)(2,1)S(1)} %split.1192), channel_id=1, source_target_pairs={{0,4},{4,0},{8,12},{12,8},{16,20},{20,16},{24,28},{28,24},{1,5},{5... | collective-permute-start | bytes 3145736 | tf_op jit(solution)/shard_map/ppermute | solution.py:48
  300.1 34.8 %collective-permute-start.36 = (bf16[256,1024]{1,0:T(8,128)(2,1)S(1)}, bf16[256,1024]{1,0:T(8,128)(2,1)S(1)}, u32[]{:S(2)}, u32[]{:S(2)}) collective-permute-start(bf16[256,1024]{1,0:T(8,128)(2,1)S(1)} %fusion.150), channel_id=1, source_target_pairs={{0,2},{2,0},{1,3},{3,1},{4,6},{6,4},{5,7},{7,5},{8,10},{10,8},{9,1... | collective-permute-start | bytes 1572872 | tf_op jit(solution)/shard_map/ppermute | solution.py:30
  312.4 32.8 %collective-permute-start.43 = (bf16[256,1024]{1,0:T(8,128)(2,1)S(1)}, bf16[256,1024]{1,0:T(8,128)(2,1)S(1)}, u32[]{:S(2)}, u32[]{:S(2)}) collective-permute-start(bf16[256,1024]{1,0:T(8,128)(2,1)S(1)} %fusion.146), channel_id=1, source_target_pairs={{0,2},{2,0},{1,3},{3,1},{4,6},{6,4},{5,7},{7,5},{8,10},{10,8},{9,1... | collective-permute-start | bytes 1572872 | tf_op jit(solution)/shard_map/ppermute | solution.py:30
  350.1 53.1 %collective-permute-start.41 = (bf16[256,1024]{1,0:T(8,128)(2,1)S(1)}, bf16[256,1024]{1,0:T(8,128)(2,1)S(1)}, u32[]{:S(2)}, u32[]{:S(2)}) collective-permute-start(bf16[256,1024]{1,0:T(8,128)(2,1)S(1)} %get-tuple-element.56), channel_id=1, source_target_pairs={{0,1},{1,0},{2,3},{3,2},{4,5},{5,4},{6,7},{7,6},{8,9},{9,8},{10,11... | collective-permute-start | bytes 1572872 | tf_op jit(solution)/shard_map/ppermute | solution.py:26
  350.1 53.1 %collective-permute-start.44 = (bf16[256,1024]{1,0:T(8,128)(2,1)S(1)}, bf16[256,1024]{1,0:T(8,128)(2,1)S(1)}, u32[]{:S(2)}, u32[]{:S(2)}) collective-permute-start(bf16[256,1024]{1,0:T(8,128)(2,1)S(1)} %get-tuple-element.88), channel_id=1, source_target_pairs={{0,1},{1,0},{2,3},{3,2},{4,5},{5,4},{6,7},{7,6},{8,9},{9,8},{10,11... | collective-permute-start | bytes 1572872 | tf_op jit(solution)/shard_map/ppermute | solution.py:26
  365.0 27.4 %collective-permute-start.67 = (bf16[128,1024]{1,0:T(8,128)(2,1)S(1)}, bf16[128,1024]{1,0:T(8,128)(2,1)S(1)}, u32[]{:S(2)}, u32[]{:S(2)}) collective-permute-start(bf16[128,1024]{1,0:T(8,128)(2,1)S(1)} %get-tuple-element.123), channel_id=1, source_target_pairs={{0,24},{4,28},{8,0},{12,4},{16,8},{20,12},{24,16},{28,20},{1,25},{... | collective-permute-start | bytes 786440 | tf_op jit(solution)/shard_map/ppermute | solution.py:48
  392.4 37.7 %collective-permute-start.37 = (bf16[256,1024]{1,0:T(8,128)(2,1)}, bf16[256,1024]{1,0:T(8,128)(2,1)}, u32[]{:S(2)}, u32[]{:S(2)}) collective-permute-start(bf16[256,1024]{1,0:T(8,128)(2,1)} %get-tuple-element.145), channel_id=1, source_target_pairs={{0,1},{1,0},{2,3},{3,2},{4,5},{5,4},{6,7},{7,6},{8,9},{9,8},{10,11... | collective-permute-start | bytes 1572872 | tf_op jit(solution)/shard_map/ppermute | solution.py:26
  402.2 27.9 %collective-permute-start.38 = (bf16[256,1024]{1,0:T(8,128)(2,1)}, bf16[256,1024]{1,0:T(8,128)(2,1)}, u32[]{:S(2)}, u32[]{:S(2)}) collective-permute-start(bf16[256,1024]{1,0:T(8,128)(2,1)} %get-tuple-element.146), channel_id=1, source_target_pairs={{0,1},{1,0},{2,3},{3,2},{4,5},{5,4},{6,7},{7,6},{8,9},{9,8},{10,11... | collective-permute-start | bytes 1572872 | tf_op jit(solution)/shard_map/ppermute | solution.py:26
  425.4 41.7 %collective-permute-start.62 = (bf16[512,1024]{0,1:T(8,128)(2,1)S(1)}, bf16[512,1024]{0,1:T(8,128)(2,1)S(1)}, u32[]{:S(2)}, u32[]{:S(2)}) collective-permute-start(bf16[512,1024]{0,1:T(8,128)(2,1)S(1)} %fusion.50), channel_id=1, source_target_pairs={{0,4},{4,0},{8,12},{12,8},{16,20},{20,16},{24,28},{28,24},{1,5},{5... | collective-permute-start | bytes 3145736 | tf_op jit(solution)/shard_map/ppermute | solution.py:48
  471.2 26.7 %collective-permute-start.64 = (bf16[128,1024]{0,1:T(8,128)(2,1)}, bf16[128,1024]{0,1:T(8,128)(2,1)S(1)}, u32[]{:S(2)}, u32[]{:S(2)}) collective-permute-start(bf16[128,1024]{0,1:T(8,128)(2,1)} %get-tuple-element.128), channel_id=1, source_target_pairs={{0,16},{4,20},{8,24},{12,28},{16,0},{20,4},{24,8},{28,12},{1,17},{... | collective-permute-start | bytes 786440 | tf_op jit(solution)/shard_map/ppermute | solution.py:48
  471.2 27.9 %collective-permute-start.65 = (bf16[128,1024]{0,1:T(8,128)(2,1)S(1)}, bf16[128,1024]{0,1:T(8,128)(2,1)S(1)}, u32[]{:S(2)}, u32[]{:S(2)}) collective-permute-start(bf16[128,1024]{0,1:T(8,128)(2,1)S(1)} %get-tuple-element.127), channel_id=1, source_target_pairs={{0,8},{4,12},{8,16},{12,20},{16,24},{20,28},{24,0},{28,4},{1,9},{5... | collective-permute-start | bytes 786440 | tf_op jit(solution)/shard_map/ppermute | solution.py:48
  475.0 26.1 %collective-permute-start.57 = (bf16[304,256]{1,0:T(8,128)(2,1)}, bf16[304,256]{1,0:T(8,128)(2,1)}, u32[]{:S(2)}, u32[]{:S(2)}) collective-permute-start(bf16[304,256]{1,0:T(8,128)(2,1)} %concatenate.460), channel_id=1, source_target_pairs={{0,28},{4,24},{8,4},{12,0},{16,12},{20,8},{24,20},{28,16},{1,29},{... | collective-permute-start | bytes 466952 | tf_op jit(solution)/shard_map/ppermute | solution.py:48
  480.8 29.4 %collective-permute-start.56 = (bf16[304,256]{1,0:T(8,128)(2,1)}, bf16[304,256]{1,0:T(8,128)(2,1)}, u32[]{:S(2)}, u32[]{:S(2)}) collective-permute-start(bf16[304,256]{1,0:T(8,128)(2,1)} %concatenate.459), channel_id=1, source_target_pairs={{0,20},{4,16},{8,28},{12,24},{16,4},{20,0},{24,12},{28,8},{1,21},{... | collective-permute-start | bytes 466952 | tf_op jit(solution)/shard_map/ppermute | solution.py:48
  (145 other events, 2428.3 us)

commit v2 on v1

v2 whole, which is shorter than its diff:
```python
import functools
import math

import jax
import jax.numpy as jnp
from jax import lax
from jax.experimental import pallas as pl
from jax.experimental.pallas import tpu as pltpu
from jax.sharding import PartitionSpec as P

HD = 64
EMB = 256

table_eps = 1e-06
norm_eps = 1e-05
bf16 = jnp.bfloat16
f32 = jnp.float32


def dot(left, right, dims=((1,), (0,))):
    return lax.dot_general(left, right, (dims, ((), ())), preferred_element_type=f32)


def after(value, *others):
    return lax.optimization_barrier((value,) + others)[0]


SWAP_CORE = [(0, 1), (1, 0), (2, 3), (3, 2)]
SWAP_X = [(0, 2), (2, 0), (1, 3), (3, 1)]


def swap_core(value):
    return lax.ppermute(value, "tensor", SWAP_CORE)


def swap_x(value):
    return lax.ppermute(value, "tensor", SWAP_X)


class Direct:
    def __init__(self, count):
        self.count, self.chain = count, count // 2
        me = lax.axis_index("dp")
        z, y = me // 2, me % 2
        self.places = [
            ((z - dz) % self.chain) * 2 + (y ^ dy) for dy in range(2) for dz in range(self.chain)
        ]

    def step(self, value, dz, dy):
        pairs = [
            (z * 2 + y, ((z + dz) % self.chain) * 2 + (y ^ dy))
            for z in range(self.chain)
            for y in range(2)
        ]
        return lax.ppermute(value, "dp", pairs)

    def spread(self, value):
        near = [value] + [self.step(value, dz, 0) for dz in range(1, self.chain)]
        return near + [self.step(value, dz, 1) for dz in range(self.chain)]

    def spread_small(self, value):
        both = jnp.stack([value, self.step(value, 0, 1)])
        rings = [both] + [self.step(both, dz, 0) for dz in range(1, self.chain)]
        return [ring[dy] for dy in range(2) for ring in rings]

    def collect(self, values):
        arrived = [values[0]]
        for k in range(1, self.count):
            dy, dz = divmod(k, self.chain)
            arrived.append(self.step(values[k], -dz, dy))
        return arrived

    def reverse(self, arrived):
        return [
            arrived[dy * self.chain + -dz % self.chain]
            for dy in range(2)
            for dz in range(self.chain)
        ]

    def gather_near(self, block, axis):
        return jnp.concatenate(
            [block] + [self.step(block, dz, 0) for dz in range(1, self.chain)], axis=axis
        )

    def gather_far(self, near, axis):
        return jnp.concatenate([near, self.step(near, 0, 1)], axis=axis)

    def scatter_far(self, whole, axis):
        near, far = jnp.split(whole, 2, axis=axis)
        return near, self.step(far.astype(bf16), 0, 1)

    def scatter_near(self, near, far, axis):
        blocks = jnp.split(near + far.astype(f32), self.chain, axis=axis)
        total = blocks[0]
        for dz in range(1, self.chain):
            total = total + self.step(blocks[dz].astype(bf16), -dz, 0).astype(f32)
        return total


class Plain:
    def __init__(self, count):
        self.count = count
        self.places = list(range(count))

    def spread(self, value):
        return list(lax.all_gather(value, "dp"))

    spread_small = spread

    def collect(self, values):
        stacked = jnp.stack(values).astype(f32)
        return [lax.psum_scatter(stacked, "dp", scatter_dimension=0, tiled=False)]

    def gather_near(self, block, axis):
        return lax.all_gather(block, "dp", axis=axis, tiled=True)

    def gather_far(self, near, axis):
        return near

    def scatter_far(self, whole, axis):
        return whole, None

    def scatter_near(self, near, far, axis):
        return lax.psum_scatter(near, "dp", scatter_dimension=axis, tiled=True)


def block_order(value, places, axis):
    size = value.shape[axis] // len(places)
    return jnp.concatenate(
        [lax.dynamic_slice_in_dim(value, place * size, size, axis) for place in places], axis=axis
    )


def split_two(value):
    high = value.astype(bf16)
    return high, (value - high.astype(f32)).astype(bf16)


def fold(value, width):
    return jnp.concatenate(jnp.split(value, value.shape[1] // width, axis=1), axis=0)


def unfold(value, count):
    return jnp.concatenate(jnp.split(value, count, axis=0), axis=1)


def permute_kernel(row_places, column_places, source, target):
    rows = source.shape[0] // row_places.shape[0]
    columns = source.shape[1] // column_places.shape[0]
    for i in range(row_places.shape[0]):
        for j in range(column_places.shape[0]):
            first = pl.multiple_of(row_places[i] * rows, rows)
            second = pl.multiple_of(column_places[j] * columns, columns)
            target[i * rows : (i + 1) * rows, j * columns : (j + 1) * columns] = source[
                pl.ds(first, rows), pl.ds(second, columns)
            ]


def permute(value, row_places, column_places):
    lists = [jnp.stack([jnp.int32(p) for p in places]) for places in (row_places, column_places)]
    return pl.pallas_call(
        permute_kernel,
        out_shape=jax.ShapeDtypeStruct(value.shape, value.dtype),
        in_specs=[pl.BlockSpec(memory_space=pltpu.SMEM)] * 2
        + [pl.BlockSpec(memory_space=pltpu.VMEM)],
        out_specs=pl.BlockSpec(memory_space=pltpu.VMEM),
        compiler_params=pltpu.CompilerParams(vmem_limit_bytes=32 << 20),
        name="permute",
    )(*lists, value)


ROWS_OF_BOTH = ((1,), (1,))
COLUMNS_OF_BOTH = ((0,), (0,))


def attention_kernel(heads, same_row, same_column, query, keys, values, attended, logsum):
    same = same_row[...] == same_column[...]
    q, k, v = query[...], keys[...], values[...]
    head = lax.broadcasted_iota(jnp.int32, q.shape, 1) // HD
    total_out = jnp.zeros(q.shape, f32)
    for h in range(heads):
        scores = dot(jnp.where(head == h, q, jnp.zeros_like(q)), k, ROWS_OF_BOTH)
        scores = jnp.where(same, scores, -1e30)
        peak = jnp.max(scores, axis=1, keepdims=True)
        expo = jnp.exp(scores - peak)
        total = jnp.sum(expo, axis=1, keepdims=True)
        total_out = jnp.where(head == h, dot(expo.astype(bf16), v) / total, total_out)
        logsum[:, h : h + 1] = peak + jnp.log(total)
    attended[...] = total_out.astype(bf16)


def attention(document, query, keys, values):
    rows, width = query.shape
    heads = width // HD
    block = min(512, rows)
    part = pl.BlockSpec((block, width), lambda i: (i, 0))
    whole = pl.BlockSpec((rows, width), lambda i: (0, 0))
    return pl.pallas_call(
        functools.partial(attention_kernel, heads),
        grid=(rows // block,),
        in_specs=[
            pl.BlockSpec((block, 1), lambda i: (i, 0)),
            pl.BlockSpec((1, rows), lambda i: (0, 0)),
            part,
            whole,
            whole,
        ],
        out_specs=[part, pl.BlockSpec((block, heads), lambda i: (i, 0))],
        out_shape=[
            jax.ShapeDtypeStruct((rows, width), bf16),
            jax.ShapeDtypeStruct((rows, heads), f32),
        ],
        compiler_params=pltpu.CompilerParams(vmem_limit_bytes=48 << 20),
        cost_estimate=pl.CostEstimate(
            flops=4 * rows * rows * width * 4, bytes_accessed=8 * rows * width, transcendentals=0
        ),
        name="attention",
    )(document[:, None], document[None, :], query, keys, values)


def attention_back_kernel(
    heads,
    count,
    same_row,
    same_column,
    query,
    keys,
    values,
    grad_attended,
    attended,
    logsum,
    grad_query,
    grad_keys,
    grad_values,
    sum_keys,
    sum_values,
):
    at = pl.program_id(0)
    same = same_row[...] == same_column[...]
    q, k, v, g = query[...], keys[...], values[...], grad_attended[...]
    head = lax.broadcasted_iota(jnp.int32, q.shape, 1) // HD
    product = g.astype(f32) * attended[...].astype(f32)

    @pl.when(at == 0)
    def _():
        sum_keys[...] = jnp.zeros_like(sum_keys)
        sum_values[...] = jnp.zeros_like(sum_values)

    out = jnp.zeros(q.shape, f32)
    for h in range(heads):
        here = head == h
        q_head = jnp.where(here, q, jnp.zeros_like(q))
        g_head = jnp.where(here, g, jnp.zeros_like(g))
        scores = jnp.where(same, dot(q_head, k, ROWS_OF_BOTH), -1e30)
        probs = jnp.exp(scores - logsum[:, h : h + 1])
        inner = jnp.sum(jnp.where(here, product, 0.0), axis=1, keepdims=True)
        grad_scores = probs * (dot(g_head, v, ROWS_OF_BOTH) - inner)
        grad_scores = grad_scores.astype(bf16)
        out = jnp.where(here, dot(grad_scores, k), out)
        sum_keys[...] += dot(grad_scores, q_head, COLUMNS_OF_BOTH)
        sum_values[...] += dot(probs.astype(bf16), g_head, COLUMNS_OF_BOTH)
    grad_query[...] = (out * (1.0 / math.sqrt(HD))).astype(bf16)

    @pl.when(at == count - 1)
    def _():
        grad_keys[...] = sum_keys[...].astype(bf16)
        grad_values[...] = sum_values[...].astype(bf16)


def attention_back(document, query, keys, values, grad_attended, attended, logsum):
    rows, width = query.shape
    heads = width // HD
    block = min(512, rows)
    part = pl.BlockSpec((block, width), lambda i: (i, 0))
    whole = pl.BlockSpec((rows, width), lambda i: (0, 0))
    return pl.pallas_call(
        functools.partial(attention_back_kernel, heads, rows // block),
        grid=(rows // block,),
        in_specs=[
            pl.BlockSpec((block, 1), lambda i: (i, 0)),
            pl.BlockSpec((1, rows), lambda i: (0, 0)),
            part,
            whole,
            whole,
            part,
            part,
            pl.BlockSpec((block, heads), lambda i: (i, 0)),
        ],
        out_specs=[part, whole, whole],
        out_shape=[jax.ShapeDtypeStruct((rows, width), bf16)] * 3,
        scratch_shapes=[pltpu.VMEM((rows, width), f32)] * 2,
        compiler_params=pltpu.CompilerParams(vmem_limit_bytes=48 << 20),
        cost_estimate=pl.CostEstimate(
            flops=10 * rows * rows * width * 4, bytes_accessed=16 * rows * width, transcendentals=0
        ),
        name="attention_back",
    )(document[:, None], document[None, :], query, keys, values, grad_attended, attended, logsum)


def norm_parts(value):
    centred = value - jnp.mean(value, axis=-1, keepdims=True)
    inverse = lax.rsqrt(jnp.mean(centred * centred, axis=-1, keepdims=True) + norm_eps)
    return centred * inverse, inverse


def norm_back(grad, normal, inverse, scale):
    inner = grad * (1.0 + scale)
    return inverse * (
        inner
        - jnp.mean(inner, axis=-1, keepdims=True)
        - normal * jnp.mean(inner * normal, axis=-1, keepdims=True)
    )


def per_device(
    token_ids,
    lengths,
    time_steps,
    embed_table,
    input_weight,
    time_weight,
    project_weight,
    output_weight,
    up_weight,
    down_weight,
    cotangent,
):
    rows = token_ids.shape[0]
    half, quarter = rows // 2, rows // 4
    count = lax.axis_size("dp")
    groups = lax.axis_size("tensor")
    me = lax.axis_index("dp")
    place = lax.axis_index("tensor")
    x, c = place // 2, place % 2
    width = cotangent.shape[1]
    docs = lengths.shape[0]
    shard = embed_table.shape[0]
    emb_rows = input_weight.shape[0]
    direct = count % 2 == 0 and count <= 8 and (width // count) % 128 == 0
    dp = Direct(count) if direct else Plain(count)
    places = dp.places
    inverse_places = [
        sum(jnp.where(jnp.int32(places[k]) == a, k, 0) for k in range(count)) for a in range(count)
    ]

    order, back_order = (places, inverse_places) if direct else ([0], [0])

    table = embed_table.astype(f32)
    rscale = lax.rsqrt(jnp.mean(table * table, axis=1, keepdims=True) + table_eps)
    normed = (table * rscale).astype(bf16)
    my_ids = lax.dynamic_slice_in_dim(token_ids, (c * 2 + x) * quarter, quarter)
    heard = dp.spread_small(jnp.concatenate([my_ids, time_steps]))
    ids = [message[:quarter] for message in heard]
    steps = jnp.concatenate([message[quarter:] for message in heard])

    pair = jnp.concatenate([normed, swap_x(normed)], axis=0)
    shards = jnp.concatenate([pair, swap_core(pair)], axis=0)
    entry = jnp.arange(4 * shard, dtype=jnp.int32)
    which = entry // shard
    owner = (x ^ (which & 1)) * 2 + (c ^ (which >> 1))
    vocab = (me * groups + owner) * shard + entry % shard

    feature = me * emb_rows + jnp.arange(emb_rows, dtype=jnp.int32)
    part = EMB // 2
    frequency = jnp.exp(-math.log(10000.0) * (feature % part).astype(f32) / part)
    angles = steps.astype(f32)[:, None] * frequency[None, :]
    features = jnp.where(feature[None, :] < part, jnp.sin(angles), jnp.cos(angles)).astype(bf16)

    head_width = project_weight.shape[1]
    heads = head_width // (3 * HD)
    per = width // count
    ordered = project_weight.reshape(per, heads, 3, HD).transpose(0, 2, 1, 3)
    ordered = ordered.reshape(per, head_width)
    project_near = dp.gather_near(after(ordered, steps), 0)
    columns = width // groups
    input_part = lax.dynamic_slice_in_dim(input_weight, place * columns, columns, 1)

    time_part = lax.dynamic_slice_in_dim(time_weight, place * width, width, 1)
    messages = []
    for k in range(count):
        onehot = (ids[k][:, None] == vocab[None, :]).astype(bf16)
        found = dot(onehot, shards).astype(bf16)
        mods = dot(features[k * docs : (k + 1) * docs], time_part)
        high, low = split_two(mods)
        small = fold(jnp.concatenate([high, low], axis=0), EMB)
        if direct:
            small = jnp.concatenate([small, fold(input_part, EMB)], axis=0)
        messages.append(jnp.concatenate([found, small], axis=0))
    arrived = dp.collect(messages)
    extra = quarter + 8 * docs
    if direct:
        input_rel = jnp.concatenate([message[extra:] for message in dp.reverse(arrived)], axis=0)
    else:
        input_rel = lax.all_gather(input_part, "dp", axis=0, tiled=True)
    arrived = sum(message[:extra].astype(f32) for message in arrived)
    project_far = dp.gather_far(after(project_near, messages[-1]), 0)
    output_near = dp.gather_near(after(output_weight, arrived), 1)
    up_near = dp.gather_near(after(up_weight, arrived), 0)
    embed_quarter = arrived[:quarter].astype(bf16)
    mods = unfold(arrived[quarter:], width // EMB)
    mods = mods[:docs] + mods[docs:]
    if direct:
        mods = block_order(mods, places, 1)
    high, low = split_two(mods)
    small = fold(jnp.concatenate([high, low], axis=0), EMB)
    mine = jnp.concatenate([embed_quarter, small, input_rel], axis=0)
    other = swap_x(mine)
    both = jnp.stack([jnp.where(x == 0, mine, other), jnp.where(x == 0, other, mine)])
    far = swap_core(both)
    embed = jnp.concatenate(
        [both[0, :quarter], far[0, :quarter], both[1, :quarter], far[1, :quarter]], axis=0
    )
    ordered = []
    for at in range(2):
        ordered.append(jnp.where(c == 0, both[at, quarter:], far[at, quarter:]))
        ordered.append(jnp.where(c == 0, far[at, quarter:], both[at, quarter:]))
    blocks = [unfold(block[: 8 * docs], width // EMB) for block in ordered]
    input_full = jnp.concatenate([block[8 * docs :] for block in ordered], axis=1)
    if direct:
        input_full = permute(input_full, inverse_places, places)
    position = jnp.concatenate(
        [
            start + jnp.arange(quarter, dtype=jnp.int32)
            for start in (c * half, (1 - c) * half, c * half + quarter, (1 - c) * half + quarter)
        ]
    )
    ends = jnp.cumsum(lengths)
    document = jnp.sum((position[:, None] >= ends[None, :]).astype(jnp.int32), axis=1)
    member = document[:, None] == jnp.arange(docs, dtype=jnp.int32)[None, :]
    member = member.astype(bf16)
    member_two = jnp.concatenate([member, member], axis=1)

    def own(value):
        return jnp.concatenate([value[:quarter], value[half : half + quarter]], axis=0)

    member_own = own(member)
    member_two_own = own(member_two)

    stream_zero = dot(embed, input_full)
    normal_one, inverse_one = norm_parts(stream_zero)
    scale_one = dot(member_two, blocks[0])
    hidden_one = (normal_one * (1.0 + scale_one) + dot(member_two, blocks[1])).astype(bf16)
    stream_zero = own(stream_zero)
    normal_one, inverse_one = norm_parts(stream_zero)

    projected = dot(hidden_one, project_far).astype(bf16)
    third = heads * HD
    query = projected[:, :third] * jnp.asarray(1.0 / math.sqrt(HD), bf16)
    keys = projected[:, third : 2 * third]
    values = projected[:, 2 * third :]
    down_near = dp.gather_near(after(down_weight, projected), 1)
    output = dp.gather_far(after(output_near, projected), 1)
    attended, logsum = attention(document, query, keys, values)
    up = dp.gather_far(after(up_near, projected), 0)

    def reduce_chunk(partial):
        mine = partial[:quarter] + swap_core(partial[quarter:].astype(bf16)).astype(f32)
        mine = mine.astype(bf16)
        return mine.astype(f32) + swap_x(mine).astype(f32)

    row_places = [2 * c, 2 * (1 - c), 2 * c + 1, 2 * (1 - c) + 1]
    cot = permute(after(cotangent, steps), row_places, order)
    attention_sum = [
        reduce_chunk(dot(attended[at * half : (at + 1) * half], output)) for at in range(2)
    ]
    stream_one, normals, inverses, scales, hidden_two = [], [], [], [], []
    for at in range(2):
        stream = stream_zero[at * quarter : (at + 1) * quarter] + attention_sum[at]
        normal, inverse = norm_parts(stream)
        members = member_two_own[at * quarter : (at + 1) * quarter]
        scale = dot(members, blocks[2])
        hidden = (normal * (1.0 + scale) + dot(members, blocks[3])).astype(bf16)
        hidden_two.append(jnp.concatenate([hidden, swap_core(hidden)], axis=0))
        stream_one.append(stream)
        normals.append(normal)
        inverses.append(inverse)
        scales.append(scale)
    down = dp.gather_far(after(down_near, attention_sum[0]), 1)
    activated, grad_upward, grad_two, branch = [], [], [], []
    for at in range(2):
        upward = dot(hidden_two[at], up)
        phi = 0.5 * (1.0 + lax.erf(upward * math.sqrt(0.5)))
        active = (upward * phi).astype(bf16)
        slope = phi + upward * (math.sqrt(0.5 / math.pi) * jnp.exp(-0.5 * upward * upward))
        grad_active = dot(cot[at * half : (at + 1) * half], down, ROWS_OF_BOTH)
        grad_up_rows = (grad_active * slope).astype(bf16)
        activated.append(active)
        grad_upward.append(grad_up_rows)
        grad_two.append(reduce_chunk(dot(grad_up_rows, up, ROWS_OF_BOTH)))
    activated = jnp.concatenate(activated, axis=0)
    grad_upward = jnp.concatenate(grad_upward, axis=0)
    hidden_two = jnp.concatenate(hidden_two, axis=0)
    grad_down = dot(activated, cot, COLUMNS_OF_BOTH)
    grad_up = dot(hidden_two, grad_upward, COLUMNS_OF_BOTH)
    down_mine, down_far = dp.scatter_far(grad_down, 1)
    branch_sent = dot(activated, down)

    grad_one, grad_attn, grad_scale_two, grad_shift_two = [], [], 0.0, 0.0
    for at in range(2):
        grad = grad_two[at]
        back = norm_back(grad, normals[at], inverses[at], scales[at])
        stream = cot[at * half : at * half + quarter].astype(f32) + back
        low = stream.astype(bf16)
        grad_attn += [low, swap_core(low)]
        grad_one.append(stream)
        members = member_own[at * quarter : (at + 1) * quarter]
        grad_scale_two += dot(members, (grad * normals[at]).astype(bf16), COLUMNS_OF_BOTH)
        grad_shift_two += dot(members, grad.astype(bf16), COLUMNS_OF_BOTH)
    grad_attn = jnp.concatenate(grad_attn, axis=0)
    if direct:
        summed_down = dp.scatter_near(down_mine, after(down_far, grad_one[0]), 1)
        up_mine, up_far = dp.scatter_far(after(grad_up, down_far, grad_one[0]), 0)
    else:
        summed_down = dp.scatter_near(down_mine, None, 1)
        up_mine, up_far = dp.scatter_far(grad_up, 0)
    grad_output = dot(attended, grad_attn, COLUMNS_OF_BOTH)
    grad_attended = dot(grad_attn, output, ROWS_OF_BOTH).astype(bf16)
    two = 2 * HD
    grad_parts = []
    for at in range(0, third, two):
        lanes = slice(at, at + two)
        grad_parts.append(
            attention_back(
                document,
                query[:, lanes],
                keys[:, lanes],
                values[:, lanes],
                grad_attended[:, lanes],
                attended[:, lanes],
                logsum[:, at // HD : at // HD + 2],
            )
        )
    grad_projected = jnp.concatenate(
        [parts[which] for which in range(3) for parts in grad_parts], axis=1
    )
    if direct:
        summed_up = dp.scatter_near(up_mine, after(up_far, grad_projected), 0)
    else:
        summed_up = dp.scatter_near(up_mine, None, 0)
    grad_hidden_one = [
        reduce_chunk(dot(grad_projected[at * half : (at + 1) * half], project_far, ROWS_OF_BOTH))
        for at in range(2)
    ]
    grad_project = dot(hidden_one, grad_projected, COLUMNS_OF_BOTH)
    if direct:
        grad_output = jnp.concatenate(
            [unfold(grad_output[:, k * per : (k + 1) * per], 2) for k in range(count)], axis=0
        )
        one_mine, one_far = dp.scatter_far(
            jnp.concatenate([grad_project, grad_output], axis=1), 0
        )
        summed_one = dp.scatter_near(one_mine, one_far, 0)
        summed_project = summed_one[:, :head_width]
        summed_output = fold(summed_one[:, head_width:], per)
    else:
        summed_project = dp.scatter_near(grad_project, None, 0)
        summed_output = dp.scatter_near(grad_output, None, 1)
    summed_project = (
        summed_project.reshape(per, 3, heads, HD).transpose(0, 2, 1, 3).reshape(per, head_width)
    )

    branch_sent = after(branch_sent, grad_hidden_one[1])
    out_blocks = []
    for at in range(2):
        branch = reduce_chunk(branch_sent[at * half : (at + 1) * half])
        block = (stream_one[at] + branch).astype(bf16)
        out_blocks += [block, swap_core(block)]
    back_places = [c, 2 + c, 1 - c, 3 - c]
    block_out = permute(jnp.concatenate(out_blocks, axis=0), back_places, back_order)

    grad = jnp.concatenate(grad_hidden_one, axis=0)
    back = norm_back(grad, normal_one, inverse_one, own(scale_one))
    grad_zero = (back + jnp.concatenate(grad_one, axis=0)).astype(bf16)
    grad_scale_one = dot(member_own, (grad * normal_one).astype(bf16), COLUMNS_OF_BOTH)
    grad_shift_one = dot(member_own, grad.astype(bf16), COLUMNS_OF_BOTH)
    grad_embed = dot(grad_zero, input_full, ROWS_OF_BOTH).astype(bf16)
    grad_embed = jnp.where(x == 0, grad_embed[:quarter], grad_embed[quarter:])
    grad_mods = jnp.concatenate(
        [grad_scale_one, grad_shift_one, grad_scale_two, grad_shift_two], axis=0
    )
    if direct:
        grad_mods = block_order(grad_mods, inverse_places, 1)
    grad_mods = grad_mods + swap_core(grad_mods)
    mod_part = lax.dynamic_slice_in_dim(grad_mods, place * docs, docs, 0).astype(bf16)
    grad_input = dot(own(embed), grad_zero, COLUMNS_OF_BOTH)
    if direct:
        grad_input = permute(grad_input, [0], inverse_places)
    mine = lax.dynamic_slice_in_dim(grad_input, place * columns, columns, 1)
    partner = lax.dynamic_slice_in_dim(grad_input, (x * 2 + 1 - c) * columns, columns, 1)
    mine = (mine + swap_core(partner.astype(bf16)).astype(f32)).astype(bf16)
    for_places = [lax.dynamic_slice_in_dim(mine, p * emb_rows, emb_rows, 0) for p in places]
    to_all = jnp.concatenate([grad_embed, fold(mod_part, EMB)], axis=0)
    if direct:
        arrived = []
        for k in range(count):
            dy, dz = divmod(k, dp.chain)
            message = jnp.concatenate([to_all, for_places[(-dz) % dp.chain + dy * dp.chain]], axis=0)
            arrived.append(message if k == 0 else dp.step(message, dz, dy))
        extra = arrived[0].shape[0] - emb_rows
        input_part = sum(message[extra:].astype(f32) for message in arrived)
    else:
        arrived = dp.spread(to_all)
        input_part = dp.collect([block.astype(f32) for block in for_places])[0]
        extra = to_all.shape[0]
    grad_tokens = jnp.concatenate([message[:quarter] for message in arrived], axis=0)
    all_mods = jnp.concatenate(
        [unfold(message[quarter:extra], width // EMB) for message in arrived], axis=0
    )
    time_grad = dot(features, all_mods, COLUMNS_OF_BOTH)
    small = jnp.concatenate([time_grad, input_part], axis=1)
    other = swap_x(small)
    both = jnp.stack([jnp.where(x == 0, small, other), jnp.where(x == 0, other, small)])
    far = swap_core(both)
    pieces = []
    for at in range(2):
        pieces += [jnp.where(c == 0, both[at], far[at]), jnp.where(c == 0, far[at], both[at])]
    summed_time = jnp.concatenate([piece[:, :width] for piece in pieces], axis=1)
    summed_input = jnp.concatenate([piece[:, width:] for piece in pieces], axis=1)

    all_ids = jnp.concatenate(ids)

    def table_part(at):
        names = vocab[at * 2 * shard : (at + 1) * 2 * shard]
        onehot = (names[:, None] == all_ids[None, :]).astype(bf16)
        return dot(onehot, grad_tokens)

    far = swap_core(table_part(1).astype(bf16))
    near = table_part(0) + far.astype(f32)
    grad_normed = near[:shard] + swap_x(near[shard:].astype(bf16)).astype(f32)
    grad_table = rscale * grad_normed - table * (
        rscale * rscale * rscale * jnp.mean(grad_normed * table, axis=1, keepdims=True)
    )
    return (
        block_out,
        grad_table,
        summed_input,
        summed_time,
        summed_project,
        summed_output,
        summed_up,
        summed_down,
    )


def solution(mesh):
    return jax.shard_map(
        per_device,
        mesh=mesh,
        in_specs=(
            P("dp"),
            P("dp"),
            P("dp"),
            P(("dp", "tensor"), None),
            P("dp", None),
            P("dp", None),
            P("dp", "tensor"),
            P("tensor", "dp"),
            P("dp", "tensor"),
            P("tensor", "dp"),
            P("dp", None),
        ),
        out_specs=(
            P("dp", None),
            P(("dp", "tensor"), None),
            P("dp", None),
            P("dp", None),
            P("dp", "tensor"),
            P("tensor", "dp"),
            P("dp", "tensor"),
            P("tensor", "dp"),
        ),
        check_vma=False,
    )
```

time: 570 us -> 489 us (0.86)
  the two profiles are of different devices: /device:TPU:0 before, /device:TPU:8 now
where the time goes in v2:
time: 489 us; the launch traced here: 480 us
  waiting for transfers between devices  196 us (40%)
  starting transfers between devices  95.6 us (20%)
  local copies, waits for them, and re-layouts  62.6 us (13%)
  matrix products  59.5 us (12%)
  other arithmetic  35 us (7%)
  Pallas kernels  27.3 us (6%)
    ppermute x46, waiting for transfers between devices, step(): return lax.ppermute(value, 'dp', pairs)  142 us
    ppermute x46, starting transfers between devices, step(): return lax.ppermute(value, 'dp', pairs)  78.5 us
    dot_general x51, matrix products, dot(): lax.dot_general(left, right, (dims, ((), ())), preferred_element_type=f32)  59.5 us
    ppermute x12, waiting for transfers between devices, swap_x(): return lax.ppermute(value, 'tensor', SWAP_X)  54.6 us
    unnamed x213, local copies, waits for them, and re-layouts  28 us
    concatenate x7, local copies, waits for them, and re-layouts, per_device(): jnp.concatenate([to_all, for_places[-dz % dp.chain + dy * dp.chain]], axi...  15 us
    pallas_call x2, Pallas kernels, attention_back(): pl.pallas_call(functools.partial(attention_back_kernel, heads, rows // bl...  14.7 us
    ppermute x12, starting transfers between devices, swap_x(): return lax.ppermute(value, 'tensor', SWAP_X)  12.6 us
  transfers between devices with their start and end apart: 78, of which 27 were waited for; matrix products, arithmetic and copies ran while one was open for 23% of the time, Pallas kernels for 6%

profile of v2, /device:TPU:8, one launch (start us, length us, event | category | flops | bytes accessed | tf_op | source)
XLA Modules:
  0.0 480.0 jit_solution(1986930147742492617)
XLA Ops:
  29.7 6.4 %collective-permute-done.17 = bf16[128,768]{0,1:T(8,128)(2,1)S(1)} collective-permute-done((bf16[128,768]{0,1:T(8,128)(2,1)S(1)}, bf16[128,768]{0,1:T(8,128)(2,1)S(1)}, u32[]{:S(2)}, u32[]{:S(2)}) %collective-permute-start.17) | collective-permute-done | bytes 196640 | tf_op jit(solution)/shard_map/ppermute | solution.py:55
  64.1 5.0 %collective-permute-start.12 = (bf16[320,256]{1,0:T(8,128)(2,1)S(1)}, bf16[320,256]{1,0:T(8,128)(2,1)S(1)}, u32[]{:S(2)}, u32[]{:S(2)}) collective-permute-start(bf16[320,256]{1,0:T(8,128)(2,1)S(1)} %get-tuple-element.255), channel_id=1, source_target_pairs={{0,12},{4,8},{8,20},{12,16},{16,28},{20,24},{24,4},{28,0},{1,13},{... | collective-permute-start | bytes 491528 | tf_op jit(solution)/shard_map/ppermute | solution.py:55
  73.0 8.3 %collective-permute-done.10 = bf16[320,256]{1,0:T(8,128)(2,1)S(1)} collective-permute-done((bf16[320,256]{1,0:T(8,128)(2,1)S(1)}, bf16[320,256]{1,0:T(8,128)(2,1)S(1)}, u32[]{:S(2)}, u32[]{:S(2)}) %collective-permute-start.10) | collective-permute-done | bytes 163872 | tf_op jit(solution)/shard_map/ppermute | solution.py:55
  92.4 6.7 %collective-permute-done.20 = bf16[256,128]{1,0:T(8,128)(2,1)S(1)} collective-permute-done((bf16[256,128]{1,0:T(8,128)(2,1)S(1)}, bf16[256,128]{1,0:T(8,128)(2,1)S(1)}, u32[]{:S(2)}, u32[]{:S(2)}) %collective-permute-start.20) | collective-permute-done | bytes 65568 | tf_op jit(solution)/shard_map/ppermute | solution.py:55
  100.0 13.4 %collective-permute-done.19 = bf16[256,128]{1,0:T(8,128)(2,1)S(1)} collective-permute-done((bf16[256,128]{1,0:T(8,128)(2,1)S(1)}, bf16[256,128]{1,0:T(8,128)(2,1)S(1)}, u32[]{:S(2)}, u32[]{:S(2)}) %collective-permute-start.19) | collective-permute-done | bytes 65568 | tf_op jit(solution)/shard_map/ppermute | solution.py:55
  116.7 16.1 %collective-permute-done.18 = bf16[512,768]{0,1:T(8,128)(2,1)S(1)} collective-permute-done((bf16[512,768]{0,1:T(8,128)(2,1)S(1)}, bf16[512,768]{0,1:T(8,128)(2,1)S(1)}, u32[]{:S(2)}, u32[]{:S(2)}) %collective-permute-start.18) | collective-permute-done | bytes 786464 | tf_op jit(solution)/shard_map/ppermute | solution.py:55
  140.9 5.3 %copy.98 = f32[1024,1024]{0,1:T(8,128)} copy(f32[1024,1024]{1,0:T(8,128)} %copy-done.15) | data formatting | bytes 8388608 | tf_op jit(solution)/shard_map/dot_general | solution.py:21
  173.6 7.7 %attention.1 = (bf16[1024,256]{1,0:T(8,128)(2,1)S(1)}, f32[1024,4]{1,0:T(8,128)S(1)}) custom-call(s32[1024,1]{1,0:T(8,128)S(1)} %copy-done.3, s32[1,1024]{1,0:T(1,128)S(1)} %bitcast.148, bf16[1024,256]{1,0:T(8,128)(2,1)S(1)} %get-tuple-element.140.query, bf16[1024,256]{1,0:T(8,128)(2,1)S(1)} %copy-done.5, bf16[1024,256]{1,0:T(8,128)(2,1)S(1)} %copy-done.4), custom_call_target="tpu_custom_call" | custom-call | flops 4294967296 | bytes 2097152 | tf_op jit(solution)/shard_map/attention/pallas_call | solution.py:198
  190.5 17.1 %collective-permute-done.29 = bf16[512,1024]{1,0:T(8,128)(2,1)S(1)} collective-permute-done((bf16[512,1024]{1,0:T(8,128)(2,1)S(1)}, bf16[512,1024]{1,0:T(8,128)(2,1)S(1)}, u32[]{:S(2)}, u32[]{:S(2)}) %collective-permute-start.29) | collective-permute-done | bytes 1048608 | tf_op jit(solution)/shard_map/ppermute | solution.py:55
  213.9 13.4 %collective-permute-done.36 = bf16[1024,512]{1,0:T(8,128)(2,1)S(1)} collective-permute-done((bf16[1024,512]{1,0:T(8,128)(2,1)S(1)}, bf16[1024,512]{1,0:T(8,128)(2,1)S(1)}, u32[]{:S(2)}, u32[]{:S(2)}) %collective-permute-start.36) | collective-permute-done | bytes 1048608 | tf_op jit(solution)/shard_map/ppermute | solution.py:55
  250.8 10.1 %collective-permute-done.41 = bf16[256,1024]{1,0:T(8,128)(2,1)S(1)} collective-permute-done((bf16[256,1024]{1,0:T(8,128)(2,1)S(1)}, bf16[256,1024]{1,0:T(8,128)(2,1)S(1)}, u32[]{:S(2)}, u32[]{:S(2)}) %collective-permute-start.41) | collective-permute-done | bytes 524320 | tf_op jit(solution)/shard_map/ppermute | solution.py:37
  261.4 9.6 %collective-permute-done.38 = bf16[256,1024]{1,0:T(8,128)(2,1)S(1)} collective-permute-done((bf16[256,1024]{1,0:T(8,128)(2,1)S(1)}, bf16[256,1024]{1,0:T(8,128)(2,1)S(1)}, u32[]{:S(2)}, u32[]{:S(2)}) %collective-permute-start.38) | collective-permute-done | bytes 524320 | tf_op jit(solution)/shard_map/ppermute | solution.py:37
  283.4 12.2 %collective-permute-done.75 = bf16[1024,128]{1,0:T(8,128)(2,1)S(1)} collective-permute-done((bf16[1024,128]{1,0:T(8,128)(2,1)S(1)}, bf16[1024,128]{1,0:T(8,128)(2,1)S(1)}, u32[]{:S(2)}, u32[]{:S(2)}) %collective-permute-start.75) | collective-permute-done | bytes 262176 | tf_op jit(solution)/shard_map/ppermute | solution.py:55
  302.2 7.3 %attention_back.2 = (bf16[1024,128]{1,0:T(8,128)(2,1)S(1)}, bf16[1024,128]{1,0:T(8,128)(2,1)S(1)}, bf16[1024,128]{1,0:T(8,128)(2,1)S(1)}) custom-call(s32[1024,1]{1,0:T(8,128)S(1)} %copy-done.3, s32[1,1024]{1,0:T(1,128)S(1)} %bitcast.149, bf16[1024,128]{1,0:T(8,128)(2,1)S(1)} %get-tuple-element.185.query, bf16[1024,128]{1,0:T(8,128)(2,1)S(1)} %copy-done.8, ...), custom_call_target="tpu_custom_call" | custom-call | flops 5368709120 | bytes 2097152 | tf_op jit(solution)/shard_map/attention_back/pallas_call | solution.py:276
  309.6 7.4 %attention_back.3 = (bf16[1024,128]{1,0:T(8,128)(2,1)S(1)}, bf16[1024,128]{1,0:T(8,128)(2,1)S(1)}, bf16[1024,128]{1,0:T(8,128)(2,1)S(1)}) custom-call(s32[1024,1]{1,0:T(8,128)S(1)} %copy-done.3, s32[1,1024]{1,0:T(1,128)S(1)} %bitcast.150, bf16[1024,128]{1,0:T(8,128)(2,1)S(1)} %get-tuple-element.184.query, bf16[1024,128]{1,0:T(8,128)(2,1)S(1)} %copy-done.6, ...), custom_call_target="tpu_custom_call" | custom-call | flops 5368709120 | bytes 2097152 | tf_op jit(solution)/shard_map/attention_back/pallas_call | solution.py:276
  331.5 5.2 %collective-permute-start.73 = (bf16[128,1024]{1,0:T(8,128)(2,1)S(1)}, bf16[128,1024]{1,0:T(8,128)(2,1)S(1)}, u32[]{:S(2)}, u32[]{:S(2)}) collective-permute-start(bf16[128,1024]{1,0:T(8,128)(2,1)S(1)} %get-tuple-element.146), channel_id=1, source_target_pairs={{0,16},{4,20},{8,24},{12,28},{16,0},{20,4},{24,8},{28,12},{1,17},{... | collective-permute-start | bytes 786440 | tf_op jit(solution)/shard_map/ppermute | solution.py:55
  336.8 7.0 %collective-permute-done.72 = bf16[128,1024]{1,0:T(8,128)(2,1)S(1)} collective-permute-done((bf16[128,1024]{1,0:T(8,128)(2,1)S(1)}, bf16[128,1024]{1,0:T(8,128)(2,1)S(1)}, u32[]{:S(2)}, u32[]{:S(2)}) %collective-permute-start.72) | collective-permute-done | bytes 262176 | tf_op jit(solution)/shard_map/ppermute | solution.py:55
  347.1 6.8 %collective-permute-done.73 = bf16[128,1024]{1,0:T(8,128)(2,1)S(1)} collective-permute-done((bf16[128,1024]{1,0:T(8,128)(2,1)S(1)}, bf16[128,1024]{1,0:T(8,128)(2,1)S(1)}, u32[]{:S(2)}, u32[]{:S(2)}) %collective-permute-start.73) | collective-permute-done | bytes 262176 | tf_op jit(solution)/shard_map/ppermute | solution.py:55
  359.7 5.0 %collective-permute-start.68 = (bf16[128,1024]{0,1:T(8,128)(2,1)}, bf16[128,1024]{0,1:T(8,128)(2,1)}, u32[]{:S(2)}, u32[]{:S(2)}) collective-permute-start(bf16[128,1024]{0,1:T(8,128)(2,1)} %get-tuple-element.149), channel_id=1, source_target_pairs={{0,16},{4,20},{8,24},{12,28},{16,0},{20,4},{24,8},{28,12},{1,17},{... | collective-permute-start | bytes 786440 | tf_op jit(solution)/shard_map/ppermute | solution.py:55
  397.9 5.8 %collective-permute-done.56 = bf16[304,256]{1,0:T(8,128)(2,1)S(1)} collective-permute-done((bf16[304,256]{1,0:T(8,128)(2,1)}, bf16[304,256]{1,0:T(8,128)(2,1)S(1)}, u32[]{:S(2)}, u32[]{:S(2)}) %collective-permute-start.56) | collective-permute-done | bytes 155680 | tf_op jit(solution)/shard_map/ppermute | solution.py:55
  410.8 6.9 %collective-permute-done.60 = bf16[304,256]{1,0:T(8,128)(2,1)S(1)} collective-permute-done((bf16[304,256]{1,0:T(8,128)(2,1)}, bf16[304,256]{1,0:T(8,128)(2,1)S(1)}, u32[]{:S(2)}, u32[]{:S(2)}) %collective-permute-start.60) | collective-permute-done | bytes 155680 | tf_op jit(solution)/shard_map/ppermute | solution.py:55
  438.6 11.9 %collective-permute-done.46 = bf16[256,1024]{1,0:T(8,128)(2,1)S(1)} collective-permute-done((bf16[256,1024]{1,0:T(8,128)(2,1)S(1)}, bf16[256,1024]{1,0:T(8,128)(2,1)S(1)}, u32[]{:S(2)}, u32[]{:S(2)}) %collective-permute-start.46) | collective-permute-done | bytes 524320 | tf_op jit(solution)/shard_map/ppermute | solution.py:37
  450.8 10.0 %collective-permute-done.49 = bf16[256,1024]{1,0:T(8,128)(2,1)S(1)} collective-permute-done((bf16[256,1024]{1,0:T(8,128)(2,1)S(1)}, bf16[256,1024]{1,0:T(8,128)(2,1)S(1)}, u32[]{:S(2)}, u32[]{:S(2)}) %collective-permute-start.49) | collective-permute-done | bytes 524320 | tf_op jit(solution)/shard_map/ppermute | solution.py:37
  468.6 9.5 %collective-permute-done.63 = bf16[1000,256]{1,0:T(8,128)(2,1)S(1)} collective-permute-done((bf16[1000,256]{1,0:T(8,128)(2,1)S(1)}, bf16[1000,256]{1,0:T(8,128)(2,1)S(1)}, u32[]{:S(2)}, u32[]{:S(2)}) %collective-permute-start.63) | collective-permute-done | bytes 512032 | tf_op jit(solution)/shard_map/ppermute | solution.py:37
  (635 shorter events, 262.2 us)
Async XLA Ops:
  56.0 25.3 %collective-permute-start.10 = (bf16[320,256]{1,0:T(8,128)(2,1)S(1)}, bf16[320,256]{1,0:T(8,128)(2,1)S(1)}, u32[]{:S(2)}, u32[]{:S(2)}) collective-permute-start(bf16[320,256]{1,0:T(8,128)(2,1)S(1)} %get-tuple-element.253), channel_id=1, source_target_pairs={{0,28},{4,24},{8,4},{12,0},{16,12},{20,8},{24,20},{28,16},{1,29},{... | collective-permute-start | bytes 491528 | tf_op jit(solution)/shard_map/ppermute | solution.py:55
  85.9 29.4 %collective-permute-start.28 = (bf16[128,1024]{1,0:T(8,128)(2,1)S(1)}, bf16[128,1024]{1,0:T(8,128)(2,1)S(1)}, u32[]{:S(2)}, u32[]{:S(2)}) collective-permute-start(bf16[128,1024]{1,0:T(8,128)(2,1)S(1)} %copy-done.41), channel_id=1, source_target_pairs={{0,24},{4,28},{8,0},{12,4},{16,8},{20,12},{24,16},{28,20},{1,25},{... | collective-permute-start | bytes 786440 | tf_op jit(solution)/shard_map/ppermute | solution.py:55
  86.1 29.3 %collective-permute-start.27 = (bf16[128,1024]{1,0:T(8,128)(2,1)S(1)}, bf16[128,1024]{1,0:T(8,128)(2,1)S(1)}, u32[]{:S(2)}, u32[]{:S(2)}) collective-permute-start(bf16[128,1024]{1,0:T(8,128)(2,1)S(1)} %copy-done.41), channel_id=1, source_target_pairs={{0,16},{4,20},{8,24},{12,28},{16,0},{20,4},{24,8},{28,12},{1,17},{... | collective-permute-start | bytes 786440 | tf_op jit(solution)/shard_map/ppermute | solution.py:55
  88.9 26.4 %collective-permute-start.26 = (bf16[128,1024]{1,0:T(8,128)(2,1)S(1)}, bf16[128,1024]{1,0:T(8,128)(2,1)S(1)}, u32[]{:S(2)}, u32[]{:S(2)}) collective-permute-start(bf16[128,1024]{1,0:T(8,128)(2,1)S(1)} %copy-done.41), channel_id=1, source_target_pairs={{0,8},{4,12},{8,16},{12,20},{16,24},{20,28},{24,0},{28,4},{1,9},{5... | collective-permute-start | bytes 786440 | tf_op jit(solution)/shard_map/ppermute | solution.py:55
  155.8 28.9 %collective-permute-start.35 = (bf16[1024,128]{1,0:T(8,128)(2,1)}, bf16[1024,128]{1,0:T(8,128)(2,1)}, u32[]{:S(2)}, u32[]{:S(2)}) collective-permute-start(bf16[1024,128]{1,0:T(8,128)(2,1)} %param.20), channel_id=1, source_target_pairs={{0,24},{4,28},{8,0},{12,4},{16,8},{20,12},{24,16},{28,20},{1,25},{... | collective-permute-start | bytes 786440 | tf_op jit(solution)/shard_map/ppermute | solution.py:55
  155.9 29.4 %collective-permute-start.34 = (bf16[1024,128]{1,0:T(8,128)(2,1)}, bf16[1024,128]{1,0:T(8,128)(2,1)}, u32[]{:S(2)}, u32[]{:S(2)}) collective-permute-start(bf16[1024,128]{1,0:T(8,128)(2,1)} %param.20), channel_id=1, source_target_pairs={{0,16},{4,20},{8,24},{12,28},{16,0},{20,4},{24,8},{28,12},{1,17},{... | collective-permute-start | bytes 786440 | tf_op jit(solution)/shard_map/ppermute | solution.py:55
  159.8 25.5 %collective-permute-start.33 = (bf16[1024,128]{1,0:T(8,128)(2,1)}, bf16[1024,128]{1,0:T(8,128)(2,1)}, u32[]{:S(2)}, u32[]{:S(2)}) collective-permute-start(bf16[1024,128]{1,0:T(8,128)(2,1)} %param.20), channel_id=1, source_target_pairs={{0,8},{4,12},{8,16},{12,20},{16,24},{20,28},{24,0},{28,4},{1,9},{5... | collective-permute-start | bytes 786440 | tf_op jit(solution)/shard_map/ppermute | solution.py:55
  181.4 26.2 %collective-permute-start.29 = (bf16[512,1024]{1,0:T(8,128)(2,1)S(1)}, bf16[512,1024]{1,0:T(8,128)(2,1)S(1)}, u32[]{:S(2)}, u32[]{:S(2)}) collective-permute-start(bf16[512,1024]{1,0:T(8,128)(2,1)S(1)} %copy-done.24), channel_id=1, source_target_pairs={{0,4},{4,0},{8,12},{12,8},{16,20},{20,16},{24,28},{28,24},{1,5},{5... | collective-permute-start | bytes 3145736 | tf_op jit(solution)/shard_map/ppermute | solution.py:55
  186.6 40.8 %collective-permute-start.36 = (bf16[1024,512]{1,0:T(8,128)(2,1)S(1)}, bf16[1024,512]{1,0:T(8,128)(2,1)S(1)}, u32[]{:S(2)}, u32[]{:S(2)}) collective-permute-start(bf16[1024,512]{1,0:T(8,128)(2,1)S(1)} %pad_maximum_fusion.10), channel_id=1, source_target_pairs={{0,4},{4,0},{8,12},{12,8},{16,20},{20,16},{24,28},{28,24},{1,5},{5... | collective-permute-start | bytes 3145736 | tf_op jit(solution)/shard_map/ppermute | solution.py:55
  189.2 23.7 %collective-permute-start.24 = (bf16[256,1024]{1,0:T(8,128)(2,1)S(1)}, bf16[256,1024]{1,0:T(8,128)(2,1)S(1)}, u32[]{:S(2)}, u32[]{:S(2)}) collective-permute-start(bf16[256,1024]{1,0:T(8,128)(2,1)S(1)} %fusion.134), channel_id=1, source_target_pairs={{0,2},{2,0},{1,3},{3,1},{4,6},{6,4},{5,7},{7,5},{8,10},{10,8},{9,1... | collective-permute-start | bytes 1572872 | tf_op jit(solution)/shard_map/ppermute | solution.py:37
  240.6 34.0 %collective-permute-start.70 = (bf16[1024,512]{1,0:T(8,128)(2,1)S(1)}, bf16[1024,512]{1,0:T(8,128)(2,1)S(1)}, u32[]{:S(2)}, u32[]{:S(2)}) collective-permute-start(bf16[1024,512]{1,0:T(8,128)(2,1)S(1)} %split.957), channel_id=1, source_target_pairs={{0,4},{4,0},{8,12},{12,8},{16,20},{20,16},{24,28},{28,24},{1,5},{5... | collective-permute-start | bytes 3145736 | tf_op jit(solution)/shard_map/ppermute | solution.py:55
  273.3 27.5 %collective-permute-start.39 = (bf16[256,1024]{1,0:T(8,128)(2,1)S(1)}, bf16[256,1024]{1,0:T(8,128)(2,1)S(1)}, u32[]{:S(2)}, u32[]{:S(2)}) collective-permute-start(bf16[256,1024]{1,0:T(8,128)(2,1)S(1)} %get-tuple-element.98), channel_id=1, source_target_pairs={{0,1},{1,0},{2,3},{3,2},{4,5},{5,4},{6,7},{7,6},{8,9},{9,8},{10,11... | collective-permute-start | bytes 1572872 | tf_op jit(solution)/shard_map/ppermute | solution.py:33
  273.3 27.5 %collective-permute-start.42 = (bf16[256,1024]{1,0:T(8,128)(2,1)S(1)}, bf16[256,1024]{1,0:T(8,128)(2,1)S(1)}, u32[]{:S(2)}, u32[]{:S(2)}) collective-permute-start(bf16[256,1024]{1,0:T(8,128)(2,1)S(1)} %get-tuple-element.132), channel_id=1, source_target_pairs={{0,1},{1,0},{2,3},{3,2},{4,5},{5,4},{6,7},{7,6},{8,9},{9,8},{10,11... | collective-permute-start | bytes 1572872 | tf_op jit(solution)/shard_map/ppermute | solution.py:33
  295.6 32.0 %collective-permute-start.71 = (bf16[512,1024]{1,0:T(8,128)(2,1)}, bf16[512,1024]{1,0:T(8,128)(2,1)}, u32[]{:S(2)}, u32[]{:S(2)}) collective-permute-start(bf16[512,1024]{1,0:T(8,128)(2,1)} %split.956), channel_id=1, source_target_pairs={{0,4},{4,0},{8,12},{12,8},{16,20},{20,16},{24,28},{28,24},{1,5},{5... | collective-permute-start | bytes 3145736 | tf_op jit(solution)/shard_map/ppermute | solution.py:55
  323.8 31.0 %collective-permute-start.66 = (bf16[512,1024]{0,1:T(8,128)(2,1)S(1)}, bf16[512,1024]{0,1:T(8,128)(2,1)S(1)}, u32[]{:S(2)}, u32[]{:S(2)}) collective-permute-start(bf16[512,1024]{0,1:T(8,128)(2,1)S(1)} %fusion.44), channel_id=1, source_target_pairs={{0,4},{4,0},{8,12},{12,8},{16,20},{20,16},{24,28},{28,24},{1,5},{5... | collective-permute-start | bytes 3145736 | tf_op jit(solution)/shard_map/ppermute | solution.py:55
  326.8 37.9 %collective-permute-start.52 = (bf16[256,1024]{1,0:T(8,128)(2,1)S(1)}, bf16[256,1024]{1,0:T(8,128)(2,1)S(1)}, u32[]{:S(2)}, u32[]{:S(2)}) collective-permute-start(bf16[256,1024]{1,0:T(8,128)(2,1)S(1)} %fusion.127), channel_id=1, source_target_pairs={{0,2},{2,0},{1,3},{3,1},{4,6},{6,4},{5,7},{7,5},{8,10},{10,8},{9,1... | collective-permute-start | bytes 1572872 | tf_op jit(solution)/shard_map/ppermute | solution.py:37
  331.5 22.4 %collective-permute-start.73 = (bf16[128,1024]{1,0:T(8,128)(2,1)S(1)}, bf16[128,1024]{1,0:T(8,128)(2,1)S(1)}, u32[]{:S(2)}, u32[]{:S(2)}) collective-permute-start(bf16[128,1024]{1,0:T(8,128)(2,1)S(1)} %get-tuple-element.146), channel_id=1, source_target_pairs={{0,16},{4,20},{8,24},{12,28},{16,0},{20,4},{24,8},{28,12},{1,17},{... | collective-permute-start | bytes 786440 | tf_op jit(solution)/shard_map/ppermute | solution.py:55
  357.5 32.1 %collective-permute-start.67 = (bf16[128,1024]{0,1:T(8,128)(2,1)}, bf16[128,1024]{0,1:T(8,128)(2,1)}, u32[]{:S(2)}, u32[]{:S(2)}) collective-permute-start(bf16[128,1024]{0,1:T(8,128)(2,1)} %get-tuple-element.147), channel_id=1, source_target_pairs={{0,24},{4,28},{8,0},{12,4},{16,8},{20,12},{24,16},{28,20},{1,25},{... | collective-permute-start | bytes 786440 | tf_op jit(solution)/shard_map/ppermute | solution.py:55
  359.7 29.9 %collective-permute-start.69 = (bf16[128,1024]{0,1:T(8,128)(2,1)}, bf16[128,1024]{0,1:T(8,128)(2,1)}, u32[]{:S(2)}, u32[]{:S(2)}) collective-permute-start(bf16[128,1024]{0,1:T(8,128)(2,1)} %get-tuple-element.148), channel_id=1, source_target_pairs={{0,8},{4,12},{8,16},{12,20},{16,24},{20,28},{24,0},{28,4},{1,9},{5... | collective-permute-start | bytes 786440 | tf_op jit(solution)/shard_map/ppermute | solution.py:55
  359.7 30.5 %collective-permute-start.68 = (bf16[128,1024]{0,1:T(8,128)(2,1)}, bf16[128,1024]{0,1:T(8,128)(2,1)}, u32[]{:S(2)}, u32[]{:S(2)}) collective-permute-start(bf16[128,1024]{0,1:T(8,128)(2,1)} %get-tuple-element.149), channel_id=1, source_target_pairs={{0,16},{4,20},{8,24},{12,28},{16,0},{20,4},{24,8},{28,12},{1,17},{... | collective-permute-start | bytes 786440 | tf_op jit(solution)/shard_map/ppermute | solution.py:55
  373.9 61.3 %collective-permute-start.45 = (bf16[256,1024]{1,0:T(8,128)(2,1)S(1)}, bf16[256,1024]{1,0:T(8,128)(2,1)S(1)}, u32[]{:S(2)}, u32[]{:S(2)}) collective-permute-start(bf16[256,1024]{1,0:T(8,128)(2,1)S(1)} %get-tuple-element.130), channel_id=1, source_target_pairs={{0,1},{1,0},{2,3},{3,2},{4,5},{5,4},{6,7},{7,6},{8,9},{9,8},{10,11... | collective-permute-start | bytes 1572872 | tf_op jit(solution)/shard_map/ppermute | solution.py:33
  373.9 61.3 %collective-permute-start.48 = (bf16[256,1024]{1,0:T(8,128)(2,1)S(1)}, bf16[256,1024]{1,0:T(8,128)(2,1)S(1)}, u32[]{:S(2)}, u32[]{:S(2)}) collective-permute-start(bf16[256,1024]{1,0:T(8,128)(2,1)S(1)} %get-tuple-element.131), channel_id=1, source_target_pairs={{0,1},{1,0},{2,3},{3,2},{4,5},{5,4},{6,7},{7,6},{8,9},{9,8},{10,11... | collective-permute-start | bytes 1572872 | tf_op jit(solution)/shard_map/ppermute | solution.py:33
  434.7 26.5 %collective-permute-start.62 = (bf16[2000,256]{1,0:T(8,128)(2,1)S(1)}, bf16[2000,256]{1,0:T(8,128)(2,1)S(1)}, u32[]{:S(2)}, u32[]{:S(2)}) collective-permute-start(bf16[2000,256]{1,0:T(8,128)(2,1)S(1)} %fusion.27), channel_id=1, source_target_pairs={{0,1},{1,0},{2,3},{3,2},{4,5},{5,4},{6,7},{7,6},{8,9},{9,8},{10,11... | collective-permute-start | bytes 3072008 | tf_op jit(solution)/shard_map/ppermute | solution.py:33
  436.8 24.0 %collective-permute-start.49 = (bf16[256,1024]{1,0:T(8,128)(2,1)S(1)}, bf16[256,1024]{1,0:T(8,128)(2,1)S(1)}, u32[]{:S(2)}, u32[]{:S(2)}) collective-permute-start(bf16[256,1024]{1,0:T(8,128)(2,1)S(1)} %get-tuple-element.127), channel_id=1, source_target_pairs={{0,2},{2,0},{1,3},{3,1},{4,6},{6,4},{5,7},{7,5},{8,10},{10,8},{9,1... | collective-permute-start | bytes 1572872 | tf_op jit(solution)/shard_map/ppermute | solution.py:37
  (136 other events, 1623.4 us)
